TPU v7x, 256 devices: a whole 4x4x8 slice. The times are simulated.
256 devices in a mesh: region: 4 (over x), comp: 64 (over z, y, core).
Axes of the slice: x: 4, y: 4, z: 8, core: 2. Of those that a mesh axis runs over, the one named last changes fastest.
Arguments:
- spectrum: float32 [1728, 1024, 128], P('comp', 'region'), may hold values from 0.2 to 2
- wind: float32 [2, 1024, 128], P(None, 'region'), may hold values from -6 to 6
- sea_table: int32 [256, 512], P('region'), may hold values from -1 to 32767, as said below
- transfer_kernel: bfloat16 [1728, 1728], replicated, may hold values from -0.15625 to 0.15625
Outputs:
- spectrum_out: float32 [1728, 1024, 128], P('comp', 'region')
Inputs may be any that keep to these rules, and one draw needn't show every extreme that they name: `sea_table`: row r * 64 + d lists first distinct cells of block d of region r (cells d * 512 to (d + 1) * 512 - 1, numbered x' * 128 + y within the region), then -1 in its other slots; each region's rows hold, in some order, 16 rows each of 512, 256, 128 and 128 listed cells, so a region holds exactly 16384 sea cells; unlisted cells are land.
All inputs are finite; a program needn't handle non-finite values.
Results may differ from a plain program's by a relative error of at most 0.0011.
Values sent between devices are 32-bit elements; how exact they have to be, the bound alone decides.
A program may use at most 128 MiB of HBM per device.

v0:
```python
import math

import jax
import jax.numpy as jnp
from jax import lax
from jax.sharding import PartitionSpec as P

NDIR = 36
NFREQ = 48
NSUB = 2


growth_rate = 0.05
wind_floor = 0.5
dissipation = 0.02
coupling = 0.5
courant_top = 0.6
ratio_log = math.log(1.1)


def padded_2(block, sides, width):
    for axis, dim in sides:
        count = lax.axis_size(axis)
        forward = [(i, i + 1) for i in range(count - 1)]
        backward = [(target, source) for source, target in forward]
        low = lax.ppermute(
            lax.slice_in_dim(block, block.shape[dim] - width, None, axis=dim), axis, forward
        )
        high = lax.ppermute(lax.slice_in_dim(block, 0, width, axis=dim), axis, backward)
        block = jnp.concatenate([low, block, high], axis=dim)
    return block


def spectral_consts(first_comp, comp_total):
    comp_ids = first_comp + jnp.arange(comp_total, dtype=jnp.int32)
    freq_number = (comp_ids // NDIR).astype(jnp.float32)
    dir_number = (comp_ids % NDIR).astype(jnp.float32)
    centre = float(NFREQ // 2)
    all_freqs = jnp.arange(NFREQ, dtype=jnp.int32).astype(jnp.float32)
    normaliser = NDIR * jnp.sum(jnp.exp((all_freqs - centre) * ratio_log))
    frequency = jnp.exp((freq_number - centre) * ratio_log)
    direction = 2.0 * math.pi * (dir_number + 0.5) / NDIR
    group_speed = courant_top * jnp.exp(-freq_number * ratio_log)
    return (frequency, jnp.cos(direction), jnp.sin(direction), group_speed, frequency / normaliser)


def upwind(wave_field, padded, sea_mask, velocity_x, velocity_y):
    west_side = padded[..., :-2, :]
    east_side = padded[..., 2:, :]
    widths = [(0, 0)] * (wave_field.ndim - 1) + [(1, 1)]
    y_padded = jnp.pad(wave_field, widths)
    south_side = y_padded[..., :-2]
    north_side = y_padded[..., 2:]
    plus_x = jnp.maximum(velocity_x, 0.0)
    minus_x = jnp.minimum(velocity_x, 0.0)
    plus_y = jnp.maximum(velocity_y, 0.0)
    minus_y = jnp.minimum(velocity_y, 0.0)
    changed = (
        wave_field
        - plus_x * (wave_field - west_side)
        - minus_x * (east_side - wave_field)
        - plus_y * (wave_field - south_side)
        - minus_y * (north_side - wave_field)
    )
    return sea_mask * changed


def source_update(points, wind_points, kernel, consts):
    frequency, cosine_dir, sine_dir, group_speed, weights = consts
    tail = (1,) * (points.ndim - 1)
    frequency = frequency.reshape((-1,) + tail)
    cosine_dir = cosine_dir.reshape((-1,) + tail)
    sine_dir = sine_dir.reshape((-1,) + tail)
    weights = weights.reshape((-1,) + tail)
    energy = jnp.sum(weights * points, axis=0)
    projection = cosine_dir * wind_points[0][None] + sine_dir * wind_points[1][None]
    growth = growth_rate * frequency * jnp.maximum(projection - wind_floor, 0.0)
    damping = -dissipation * (frequency * frequency) * (energy * energy)[None]
    coupled = lax.dot_general(
        kernel,
        points.astype(jnp.bfloat16),
        (((1,), (0,)), ((), ())),
        preferred_element_type=jnp.float32,
    )
    change = (growth + damping) * points + coupling * points * coupled
    return points + change / (1.0 - damping)


def block_marks(sea_rows, block_rows, rows_y):
    block_cells = block_rows * rows_y
    cell_grid = (
        jnp.arange(block_rows, dtype=jnp.int32)[:, None] * rows_y
        + jnp.arange(rows_y, dtype=jnp.int32)[None, :]
    )
    slot_numbers = jnp.arange(block_cells, dtype=jnp.int32)[:, None, None]

    def one_block(inputs):
        listed, block_base = inputs
        matches = (listed - block_base)[:, None, None] == cell_grid[None]
        present = jnp.any(matches, axis=0)
        slot = jnp.max(jnp.where(matches, slot_numbers, -1), axis=0)
        return (present, slot)

    bases = jnp.arange(sea_rows.shape[0], dtype=jnp.int32) * block_cells
    present, slot = lax.map(one_block, (sea_rows, bases))
    return (present.reshape(-1, rows_y), slot)


def on_device(spectrum, wind, sea_table, transfer_kernel):
    comp_count = lax.axis_size("comp")
    comp_index = lax.axis_index("comp")
    comp_local, rows_x, rows_y = spectrum.shape
    block_rows = rows_x // comp_count
    spectral = comp_local * comp_count
    present, slot = block_marks(sea_table, block_rows, rows_y)
    sea_mask = present.astype(jnp.float32)
    frequency, cosine_dir, sine_dir, group_speed, weights = spectral_consts(
        comp_index * comp_local, comp_local
    )
    velocity_x = (group_speed * cosine_dir)[:, None, None]
    velocity_y = (group_speed * sine_dir)[:, None, None]
    wave_field = sea_mask[None] * spectrum
    for substep in range(NSUB):
        padded = padded_2(wave_field, (("region", 1),), 1)
        wave_field = upwind(wave_field, padded, sea_mask, velocity_x, velocity_y)
    consts = spectral_consts(0, spectral)
    received = lax.all_to_all(wave_field, "comp", split_axis=1, concat_axis=0, tiled=True)
    wind_points = lax.dynamic_slice_in_dim(wind, comp_index * block_rows, block_rows, 1)
    updated = source_update(received, wind_points, transfer_kernel, consts)
    result = lax.all_to_all(updated, "comp", split_axis=0, concat_axis=1, tiled=True)
    return result


def solution(mesh):
    placed = (P("comp", "region", None), P(None, "region", None), P("region", None), P())
    return jax.shard_map(
        on_device, mesh=mesh, in_specs=placed, out_specs=P("comp", "region", None), check_vma=False
    )
```

profile of v0, /device:TPU:1, one launch (start us, length us, event | category | flops | bytes accessed | tf_op | source)
XLA Modules:
  0.0 398.9 jit_solution(7573334256299383666)
XLA Ops:
  0.0 140.0 %while.11 = (s32[]{:T(128)}, pred[64,4,128]{2,1,0:T(4,128)(4,1)S(1)}, s32[64,512]{1,0:T(8,128)}, s32[64]{0:T(128)S(1)}, s32[4]{0:T(128)S(1)}, /*index=5*/s32[]{:T(128)}) while((s32[]{:T(128)}, pred[64,4,128]{2,1,0:T(4,128)(4,1)S(1)}, s32[64,512]{1,0:T(8,128)}, s32[64]{0:T(128)S(1)}, s32[4]{0:T(128)S(1)}, /*index=5*/s32[]{:T(128)}) %tuple.29), condition=%wide.region_2.3_spmd.clone, body=%wide.region_0.2_spmd.clone.sunk | while | flops 524802 | bytes 11885 | solution.py:105
  5.0 1.3 dynamic-slice_subtract_fusion.2
  9.4 1.3 dynamic-slice_subtract_fusion.2
  13.7 1.3 dynamic-slice_subtract_fusion.2
  15.9 1.3 dynamic-slice_subtract_fusion.2
  20.3 1.3 dynamic-slice_subtract_fusion.2
  24.7 1.3 dynamic-slice_subtract_fusion.2
  140.1 4.1 %copy_multiply_fusion = f32[27,256,128]{2,0,1:T(8,128)S(1)} fusion(f32[27,256,128]{2,1,0:T(8,128)} %param.6, f32[256,128]{1,0:T(8,128)S(1)} %bitcast.37), kind=kLoop, calls=%fused_computation.43 | loop fusion | flops 884736 | bytes 7208960 | tf_op jit(solution)/shard_map/mul | solution.py:122
  144.2 1.9 copy-done
  146.1 3.9 collective-permute-start
  150.0 1.3 collective-permute-start.1
  151.5 3.0 collective-permute-done.1
  154.5 11.3 %fusion.8 = f32[27,256,128]{2,0,1:T(8,128)S(1)} fusion(f32[27,256,128]{2,0,1:T(8,128)} %copy-done, f32[27,1,128]{2,0,1:T(8,128)S(1)} %collective-permute-done.1, f32[27,1,128]{2,0,1:T(8,128)S(1)} %collective-permute-done, f32[27]{0:T(128)S(1)} %get-tuple-element.64, f32[27]{0:T(128)S(1)} %get-tuple-element.65, f32[27]{0:T(128)S(1)} %get-tuple-element.66, ...), kind=kLoop, calls=%fused_computation.17 | loop fusion | flops 13271040 | bytes 7237040 | tf_op jit(solution)/shard_map/mul | solution.py:65
  165.8 3.1 collective-permute-start.2
  169.0 1.3 collective-permute-start.3
  170.3 3.2 collective-permute-done.3
  173.4 5.0 %fusion.15 = f32[27,256,128]{2,0,1:T(8,128)} fusion(f32[27,256,128]{2,0,1:T(8,128)S(1)} %fusion.8, f32[27,1,128]{2,0,1:T(8,128)S(1)} %collective-permute-done.3, f32[27,1,128]{2,0,1:T(8,128)S(1)} %collective-permute-done.2, f32[27]{0:T(128)S(1)} %get-tuple-element.64, f32[27]{0:T(128)S(1)} %get-tuple-element.65, f32[27]{0:T(128)S(1)} %get-tuple-element.66, ...), kind=kLoop, calls=%fused_computation.24 | loop fusion | flops 13271040 | bytes 7237040 | tf_op jit(solution)/shard_map/mul | solution.py:65
  178.5 15.4 %all-to-all-start = ((f32[27,256,128]{2,0,1:T(8,128)}), f32[27,256,128]{2,0,1:T(8,128)}, u32[]{:S(2)}, u32[]{:S(2)}) async-start(f32[27,256,128]{2,0,1:T(8,128)} %fusion.15), calls=%async_computation | async-start | bytes 8388608 | tf_op jit(solution)/shard_map/all_to_all | solution.py:127
  196.0 92.3 %all-to-all-done = f32[27,256,128]{2,0,1:T(8,128)} async-done(((f32[27,256,128]{2,0,1:T(8,128)}), f32[27,256,128]{2,0,1:T(8,128)}, u32[]{:S(2)}, u32[]{:S(2)}) %all-to-all-start) | async-done | bytes 3538976 | tf_op jit(solution)/shard_map/all_to_all | solution.py:127
  288.2 5.3 %fusion.34 = (f32[4,128]{1,0:T(4,128)S(1)}, f32[27,64,4,128]{3,2,0,1:T(4,128)S(1)}) fusion(f32[64,27]{1,0:T(8,128)S(1)} %fusion.41, f32[27,64,4,128]{3,0,2,1:T(8,128)} %bitcast.1), kind=kLoop, calls=%fused_computation.50 | loop fusion | flops 1768960 | bytes 7086848 | tf_op jit(solution)/shard_map/reduce_sum | solution.py:75
  293.6 6.9 %fusion.33 = f32[1728,4,128]{2,0,1:T(8,128)S(1)} fusion(f32[1728,4,128]{2,1,0:T(4,128)S(1)} %bitcast.36, bf16[1728,1728]{1,0:T(8,128)(2,1)} %param.9, f32[4,128]{1,0:T(4,128)S(1)} %mul.338, f32[1728]{0:T(1024)S(1)} %get-tuple-element.70, f32[4,128]{1,0:T(4,128)S(1)} %get-tuple-element.63, f32[1728]{0:T(1024)S(1)} %get-tuple-element.68, ...), kind=kOutput, calls=%fused_computation.47 | convolution fusion | flops 3071803392 | bytes 13083648 | tf_op jit(solution)/shard_map/dot_general | solution.py:79
  300.5 7.3 %copy.34 = f32[1728,4,128]{2,1,0:T(4,128)S(1)} copy(f32[1728,4,128]{2,0,1:T(8,128)S(1)} %fusion.33) | data formatting | bytes 7077888 | tf_op jit(solution)/shard_map/add | solution.py:86
  307.8 88.3 %all_to_all.36 = f32[1728,4,128]{2,1,0:T(4,128)S(1)} all-to-all(f32[1728,4,128]{2,1,0:T(4,128)S(1)} %copy.34), channel_id=1, replica_groups=mesh['region'=4,'comp'=64] {'comp'}, dimensions={0} | all-to-all | bytes 7077888 | tf_op jit(solution)/shard_map/all_to_all | solution.py:130
  396.2 2.8 copy.35
  (331 shorter events, 132.5 us)
Async XLA Ops:
  144.1 1.9 copy-start
  146.1 5.4 %collective-permute-start = (f32[27,1,128]{2,0,1:T(8,128)S(1)}, f32[27,1,128]{2,0,1:T(8,128)S(1)}, u32[]{:S(2)}, u32[]{:S(2)}) collective-permute-start(f32[27,1,128]{2,0,1:T(8,128)S(1)} %get-tuple-element.60), channel_id=1, source_target_pairs={{0,64},{64,128},{128,192},{1,65},{65,129},{129,193},{2,66},{66,130... | collective-permute-start | bytes 41480 | tf_op jit(solution)/shard_map/ppermute | solution.py:26
  150.0 4.5 %collective-permute-start.1 = (f32[27,1,128]{2,0,1:T(8,128)S(1)}, f32[27,1,128]{2,0,1:T(8,128)S(1)}, u32[]{:S(2)}, u32[]{:S(2)}) collective-permute-start(f32[27,1,128]{2,0,1:T(8,128)S(1)} %get-tuple-element.61), channel_id=1, source_target_pairs={{64,0},{128,64},{192,128},{65,1},{129,65},{193,129},{66,2},{130,66... | collective-permute-start | bytes 41480 | tf_op jit(solution)/shard_map/ppermute | solution.py:29
  165.8 4.4 %collective-permute-start.2 = (f32[27,1,128]{2,0,1:T(8,128)S(1)}, f32[27,1,128]{2,0,1:T(8,128)S(1)}, u32[]{:S(2)}, u32[]{:S(2)}) collective-permute-start(f32[27,1,128]{2,0,1:T(8,128)S(1)} %get-tuple-element.58), channel_id=1, source_target_pairs={{0,64},{64,128},{128,192},{1,65},{65,129},{129,193},{2,66},{66,130... | collective-permute-start | bytes 41480 | tf_op jit(solution)/shard_map/ppermute | solution.py:26
  169.0 4.5 %collective-permute-start.3 = (f32[27,1,128]{2,0,1:T(8,128)S(1)}, f32[27,1,128]{2,0,1:T(8,128)S(1)}, u32[]{:S(2)}, u32[]{:S(2)}) collective-permute-start(f32[27,1,128]{2,0,1:T(8,128)S(1)} %get-tuple-element.59), channel_id=1, source_target_pairs={{64,0},{128,64},{192,128},{65,1},{129,65},{193,129},{66,2},{130,66... | collective-permute-start | bytes 41480 | tf_op jit(solution)/shard_map/ppermute | solution.py:29
  178.5 109.8 %all-to-all-start = ((f32[27,256,128]{2,0,1:T(8,128)}), f32[27,256,128]{2,0,1:T(8,128)}, u32[]{:S(2)}, u32[]{:S(2)}) async-start(f32[27,256,128]{2,0,1:T(8,128)} %fusion.15), calls=%async_computation | async-start | bytes 8388608 | tf_op jit(solution)/shard_map/all_to_all | solution.py:127
where the time goes:
time: 406 us; the launch traced here: 399 us
  other arithmetic  127 us (31%)
  waiting for transfers between devices  98.5 us (24%)
  blocking collectives  88.3 us (22%)
  local copies, waits for them, and re-layouts  50.7 us (12%)
  starting transfers between devices  25 us (6%)
  matrix products  6.86 us (2%)
    all_to_all x1, waiting for transfers between devices, on_device(): lax.all_to_all(wave_field, 'comp', split_axis=1, concat_axis=0, tiled=True)  92.3 us
    all_to_all x1, blocking collectives, on_device(): lax.all_to_all(updated, 'comp', split_axis=0, concat_axis=1, tiled=True)  88.3 us
    sub x64, other arithmetic, one_block(): matches = (listed - block_base)[:, None, None] == cell_grid[None]  82.2 us
    dynamic_slice x64, local copies, waits for them, and re-layouts, block_marks(): present, slot = lax.map(one_block, (sea_rows, bases))  37.1 us
    mul x2, other arithmetic, upwind(): return sea_mask * changed  16.3 us
    all_to_all x1, starting transfers between devices, on_device(): lax.all_to_all(wave_field, 'comp', split_axis=1, concat_axis=0, tiled=True)  15.4 us
    reduce_or x64, other arithmetic, one_block(): present = jnp.any(matches, axis=0)  14 us
  transfers between devices with their start and end apart: 5, of which 3 were waited for; matrix products, arithmetic and copies ran while one was open for 0% of the time, Pallas kernels for 0%

commit v1 on v0

v1 whole, which is shorter than its diff:
```python
import functools
import math

import jax
import jax.numpy as jnp
import numpy as np
from jax import lax
from jax.experimental import pallas as pl
from jax.experimental.pallas import tpu as pltpu
from jax.sharding import PartitionSpec as P

NDIR = 36
NFREQ = 48
SPEC = NDIR * NFREQ
COMPS = 64
LOCAL = SPEC // COMPS
REGIONS = 4
ROWS = 256
LANES = 128
UNITS = 128
BLOCKS = 64
PADDED_ROWS = ROWS + 8
PADDED_COMP = 32
PADDED_SPEC = SPEC + 32
TILE = 432
F32 = jnp.float32
MESH = pl.DeviceIdType.MESH

growth_rate = 0.05
wind_floor = 0.5
dissipation = 0.02
coupling = 0.5
courant_top = 0.6


def component_table():
    comp = np.arange(SPEC)
    freq, direction = comp // NDIR, 2.0 * math.pi * (comp % NDIR + 0.5) / NDIR
    omega = 1.1 ** (freq - NFREQ // 2)
    speed = courant_top * 1.1 ** (-freq.astype(np.float64))
    cosine, sine = np.cos(direction), np.sin(direction)
    u, v = speed * cosine, speed * sine
    centre = 1.0 - np.abs(u) - np.abs(v)
    columns = [omega, cosine, sine, centre, np.maximum(u, 0), np.maximum(-u, 0), np.maximum(v, 0), np.maximum(-v, 0)]
    table = np.zeros((SPEC, LANES), np.float32)
    for lane, column in enumerate(columns):
        table[:, lane] = column
    return table.reshape(COMPS, LOCAL, LANES)


def energy_scale():
    return float(1.0 / (NDIR * np.sum(1.1 ** (np.arange(NFREQ) - NFREQ // 2.0))))


def shifted(me, step):
    z = (me // 8 + step // 8) % 8
    y = ((me // 2) % 4 + (step // 2) % 4) % 4
    core = (me % 2 + step % 2) % 2
    return z * 8 + y * 2 + core


def gathered(source, lanes):
    return jnp.take_along_axis(source, lanes, axis=1, mode="promise_in_bounds")


def exchange_kernel(
    spectrum, wind_field, sea_table, transfer, table,
    compact, lane_map, part_map, unit_rows,
    natural, wind, wave0, wave1, wave2, mask, sea_rows, units_smem,
    kernel_buf, constants, own, omega, cosine, sine,
    outgoing, incoming, dense, rounded, coupled, returning,
    load_sem, halo_send, halo_recv, send_sem, forward_sem, back_sem, self_sem,
):
    me = lax.axis_index("comp")
    region = lax.axis_index("region")
    west = (region + REGIONS - 1) % REGIONS
    east = (region + 1) % REGIONS

    load_spectrum = pltpu.make_async_copy(spectrum, natural.at[pl.ds(0, LOCAL * ROWS)], load_sem.at[0])
    load_spectrum.start()
    load_own = pltpu.make_async_copy(table.at[me], own, load_sem.at[1])
    load_own.start()
    load_constants = pltpu.make_async_copy(table, constants, load_sem.at[2])
    load_constants.start()
    load_kernel = pltpu.make_async_copy(transfer, kernel_buf, load_sem.at[3])
    load_kernel.start()

    load_wind = pltpu.make_async_copy(wind_field, wind.at[pl.ds(0, 2 * ROWS)], load_sem.at[5])
    load_wind.start()

    barrier = pltpu.get_barrier_semaphore()

    @pl.loop(1, COMPS)
    def _(step):
        pl.semaphore_signal(barrier, inc=1, device_id={"comp": shifted(me, step)}, device_id_type=MESH)

    pl.semaphore_signal(barrier, inc=1, device_id={"region": west}, device_id_type=MESH)
    pl.semaphore_signal(barrier, inc=1, device_id={"region": east}, device_id_type=MESH)

    for part in range(4):
        sea_rows[pl.ds(part, BLOCKS, stride=4), :] = sea_table[:, part * LANES : (part + 1) * LANES]

    listed = sea_rows[0:ROWS, :] >= 0
    held = jnp.where(listed, 1.0, 0.0).astype(jnp.bfloat16)
    lower = jnp.where(
        lax.broadcasted_iota(jnp.int32, (ROWS, ROWS), 0) > lax.broadcasted_iota(jnp.int32, (ROWS, ROWS), 1), 1.0, 0.0
    ).astype(jnp.bfloat16)
    rank = jnp.dot(lower, held, preferred_element_type=F32)
    unit = lax.broadcasted_iota(jnp.int32, (ROWS, UNITS), 1).astype(F32)
    row_number = lax.broadcasted_iota(jnp.int32, (ROWS, UNITS), 0).astype(F32)
    found = jnp.where((rank == unit) & listed, row_number, 0.0)
    unit_rows[...] = jnp.broadcast_to(jnp.sum(found, axis=0, keepdims=True), (8, UNITS)).astype(jnp.int32)
    load_units = pltpu.make_async_copy(unit_rows, units_smem, load_sem.at[4])
    load_units.start()

    lane_number = lax.broadcasted_iota(jnp.int32, (LANES, 4 * LANES), 0)
    slot = lax.broadcasted_iota(jnp.int32, (1, 4 * LANES), 1)
    slot_lane = (slot % LANES).astype(F32)
    slot_part = (slot // LANES).astype(F32)
    quarter = lax.broadcasted_iota(jnp.int32, (8, 4 * LANES), 0)

    @pl.loop(0, BLOCKS, unroll=8)
    def _(block):
        cells = sea_table[pl.ds(block, 1), :]
        lane = jnp.where(cells >= 0, cells % LANES, -1)
        inside = jnp.where(cells >= 0, (cells // LANES) % 4, -1)
        match = jnp.where(lane == lane_number, 1.0, 0.0).astype(jnp.bfloat16)
        row = jnp.where(inside == quarter, 1.0, 0.0)
        rows = jnp.concatenate([row, row * slot_lane, row * slot_part], axis=0).astype(jnp.bfloat16)
        maps = lax.dot_general(rows, match, (((1,), (1,)), ((), ())), preferred_element_type=F32)
        target = pl.ds(pl.multiple_of(block * 4, 4), 4)
        present = maps[0:4]
        mask[target, :] = present
        lane_map[target, :] = maps[8:12].astype(jnp.int32)
        part_map[target, :] = jnp.where(present > 0.5, maps[16:20], -1.0).astype(jnp.int32)

    load_own.wait()
    coefficients = own[...]
    lanes = lax.broadcasted_iota(jnp.int32, (LOCAL, LANES), 1)

    def column(number):
        return jnp.broadcast_to(coefficients[:, number : number + 1], (LOCAL, LANES))

    centre_w, west_w, east_w = column(3), column(4), column(5)
    south_w = jnp.where(lanes == 0, 0.0, column(6))
    north_w = jnp.where(lanes == LANES - 1, 0.0, column(7))

    def mask_row(x):
        return jnp.broadcast_to(mask[pl.ds(x, 1), :], (LOCAL, LANES))

    def first(x):
        wave0[x + 1] = mask_row(x) * natural[pl.ds(x, LOCAL, stride=ROWS), :]

    def substep(source, target, shift, x):
        here = source[x + 1]
        changed = (
            centre_w * here
            + west_w * source[x]
            + east_w * source[x + 2]
            + south_w * pltpu.roll(here, 1, 1)
            + north_w * pltpu.roll(here, LANES - 1, 1)
        )
        target[x + shift] = mask_row(x) * changed

    def halo(wave, number):
        to_west = pltpu.make_async_remote_copy(
            wave.at[1], wave.at[ROWS + 1], halo_send.at[2 * number], halo_recv.at[2 * number],
            device_id={"region": west}, device_id_type=MESH)
        to_east = pltpu.make_async_remote_copy(
            wave.at[ROWS], wave.at[0], halo_send.at[2 * number + 1], halo_recv.at[2 * number + 1],
            device_id={"region": east}, device_id_type=MESH)
        to_west.start()
        to_east.start()
        return to_west, to_east

    def arrived(wave, copies):
        for copy in copies:
            copy.wait()
        wave[0] = jnp.where(region > 0, wave[0], 0.0)
        wave[ROWS + 1] = jnp.where(region < REGIONS - 1, wave[ROWS + 1], 0.0)

    load_spectrum.wait()
    first(0)
    first(ROWS - 1)
    pl.semaphore_wait(barrier, COMPS + 1)
    copies = halo(wave0, 0)

    @pl.loop(1, ROWS - 1, unroll=8)
    def _(x):
        first(x)

    @pl.loop(1, ROWS - 1, unroll=8)
    def _(x):
        substep(wave0, wave1, 1, x)

    arrived(wave0, copies)
    substep(wave0, wave1, 1, 0)
    substep(wave0, wave1, 1, ROWS - 1)
    copies = halo(wave1, 1)

    @pl.loop(1, ROWS - 1, unroll=8)
    def _(x):
        substep(wave1, wave2, 0, x)

    arrived(wave1, copies)
    substep(wave1, wave2, 0, 0)
    substep(wave1, wave2, 0, ROWS - 1)

    load_units.wait()

    def unit_cells(number):
        row = jnp.clip(units_smem[0, number], 0, ROWS - 1)
        cells = sea_rows[pl.ds(row, 1), :]
        return row & ~3, cells & (LANES - 1), (cells >> 7) & 3

    def packed(number):
        base, lane, inside = unit_cells(number)
        lane = jnp.broadcast_to(lane, (LOCAL, LANES))
        inside = jnp.broadcast_to(inside, (LOCAL, LANES))
        total = gathered(wave2[base], lane)
        for quarter in range(1, 4):
            total = jnp.where(inside == quarter, gathered(wave2[base + quarter], lane), total)
        return total

    def forward(chunk, target):
        return pltpu.make_async_remote_copy(
            outgoing.at[2 * target + chunk], incoming.at[chunk, me], send_sem.at[0], forward_sem.at[chunk, me],
            device_id={"comp": target}, device_id_type=MESH)

    for chunk in range(2):

        @pl.loop(1, COMPS)
        def _(step, chunk=chunk):
            target = shifted(me, step)
            outgoing[2 * target + chunk] = packed(2 * target + chunk)
            forward(chunk, target).start()

    for chunk in range(2):
        incoming[chunk, me] = packed(2 * me + chunk)

    load_constants.wait()

    @pl.loop(0, COMPS, unroll=4)
    def _(source):
        values = constants[source]
        omega[source] = jnp.broadcast_to(values[:, 0:1], (LOCAL, LANES))
        cosine[source] = jnp.broadcast_to(values[:, 1:2], (LOCAL, LANES))
        sine[source] = jnp.broadcast_to(values[:, 2:3], (LOCAL, LANES))

    load_kernel.wait()
    load_wind.wait()

    def wind_at(chunk):
        base, lane, inside = unit_cells(2 * me + chunk)
        lane = jnp.broadcast_to(lane, (8, LANES))
        parts = []
        for part in range(2):
            total = jnp.zeros((8, LANES), F32)
            for quarter in range(4):
                line = jnp.broadcast_to(wind[pl.ds(part * ROWS + base + quarter, 1), :], (8, LANES))
                total = jnp.where(inside == quarter, gathered(line, lane), total)
            parts.append(total[0:1])
        return parts

    def back(chunk, target):
        return pltpu.make_async_remote_copy(
            returning.at[chunk, target], compact.at[2 * me + chunk], send_sem.at[1], back_sem.at[chunk, me],
            device_id={"comp": target}, device_id_type=MESH)

    for chunk in range(2):

        @pl.loop(1, COMPS)
        def _(step, chunk=chunk):
            source = shifted(me, step)
            pltpu.make_async_remote_copy(
                outgoing.at[0], incoming.at[chunk, source], send_sem.at[0], forward_sem.at[chunk, source],
                device_id={"comp": source}, device_id_type=MESH).wait_recv()

        wind_u, wind_v = wind_at(chunk)

        def collect(source, total, chunk=chunk):
            values = incoming[chunk, source]
            dense[pl.ds(source * LOCAL, LOCAL), :] = values
            return total + omega[source] * values

        total = lax.fori_loop(0, COMPS, collect, jnp.zeros((LOCAL, LANES), F32), unroll=True)
        energy = jnp.sum(total, axis=0, keepdims=True) * energy_scale()
        loss = dissipation * energy * energy
        rounded[...] = dense[0:SPEC, :].astype(jnp.bfloat16)

        @pl.loop(0, SPEC // TILE)
        def _(tile):
            rows = pl.ds(pl.multiple_of(tile * TILE, TILE), TILE)
            coupled[rows, :] = jnp.dot(kernel_buf[rows, :], rounded[...], preferred_element_type=F32)

        def updated(target, chunk=chunk, wind_u=wind_u, wind_v=wind_v, loss=loss):
            points = incoming[chunk, target]
            speed = omega[target]
            along = cosine[target] * wind_u + sine[target] * wind_v
            growth = growth_rate * speed * jnp.maximum(along - wind_floor, 0.0)
            damping = speed * speed * loss
            joined = coupled[pl.ds(target * LOCAL, LOCAL), :]
            return points + points * (growth - damping + coupling * joined) / (1.0 + damping)

        @pl.loop(1, COMPS)
        def _(step, chunk=chunk, updated=updated):
            target = shifted(me, step)
            returning[chunk, target] = updated(target)
            back(chunk, target).start()

        returning[chunk, me] = updated(me)
        pltpu.make_async_copy(returning.at[chunk, me], compact.at[2 * me + chunk], self_sem.at[chunk]).start()

    for chunk in range(2):

        @pl.loop(1, COMPS)
        def _(step, chunk=chunk):
            source = shifted(me, step)
            pltpu.make_async_remote_copy(
                returning.at[chunk, source], compact.at[2 * source + chunk], send_sem.at[1], back_sem.at[chunk, source],
                device_id={"comp": source}, device_id_type=MESH).wait_recv()

        pltpu.make_async_copy(returning.at[chunk, me], compact.at[2 * me + chunk], self_sem.at[chunk]).wait()

    for number in range(2):
        sent = outgoing.at[pl.ds(0, 2 * COMPS - 2)]
        pltpu.make_async_copy(sent, sent, send_sem.at[number]).wait()


def expand_kernel(compact, lane_map, part_map, units, result, spread, store_sem):
    @pl.loop(0, UNITS // 4)
    def _(group):
        pieces = []
        for offset in range(4):
            number = group * 4 + offset
            row = jnp.clip(units[0, number], 0, ROWS - 1)
            base, part = row & ~3, row & 3
            slots = compact[number]
            for quarter in range(4):
                line = pl.ds(base + quarter, 1)
                lane = jnp.broadcast_to(lane_map[line, :], (LOCAL, LANES))
                here = jnp.broadcast_to(part_map[line, :], (LOCAL, LANES)) == part
                pieces.append((base + quarter, part, here, gathered(slots, lane)))
        for line, part, here, values in pieces:
            target = pl.ds(line, LOCAL, stride=ROWS)
            before = jnp.where(part == 0, 0.0, spread[target, :])
            spread[target, :] = jnp.where(here, values, before)

    store = pltpu.make_async_copy(spread.at[pl.ds(0, LOCAL * ROWS)], result, store_sem)
    store.start()
    store.wait()


def on_device(spectrum, wind, sea_table, transfer_kernel):
    table = jnp.asarray(component_table())
    vmem = pl.BlockSpec(memory_space=pltpu.VMEM)
    anywhere = pl.BlockSpec(memory_space=pl.ANY)
    wave = pltpu.VMEM((ROWS + 2, LOCAL, LANES), F32)
    per_source = pltpu.VMEM((COMPS, LOCAL, LANES), F32)
    dma = pltpu.SemaphoreType.DMA
    shape = jax.ShapeDtypeStruct
    compact, lane_map, part_map, unit_rows = pl.pallas_call(
        exchange_kernel,
        out_shape=(
            shape((UNITS, LOCAL, LANES), F32),
            shape((PADDED_ROWS, LANES), jnp.int32),
            shape((PADDED_ROWS, LANES), jnp.int32),
            shape((8, UNITS), jnp.int32),
        ),
        in_specs=[anywhere, anywhere, vmem, anywhere, anywhere],
        out_specs=(anywhere, vmem, vmem, vmem),
        scratch_shapes=[
            pltpu.VMEM((PADDED_COMP * ROWS, LANES), F32),
            pltpu.VMEM((2 * ROWS + 8, LANES), F32),
            wave,
            wave,
            pltpu.VMEM((ROWS, LOCAL, LANES), F32),
            pltpu.VMEM((PADDED_ROWS, LANES), F32),
            pltpu.VMEM((PADDED_ROWS, LANES), jnp.int32),
            pltpu.SMEM((8, UNITS), jnp.int32),
            pltpu.VMEM((SPEC, SPEC), jnp.bfloat16),
            per_source,
            pltpu.VMEM((LOCAL, LANES), F32),
            per_source,
            per_source,
            per_source,
            pltpu.VMEM((UNITS, LOCAL, LANES), F32),
            pltpu.VMEM((2, COMPS, LOCAL, LANES), F32),
            pltpu.VMEM((PADDED_SPEC, LANES), F32),
            pltpu.VMEM((SPEC, LANES), jnp.bfloat16),
            pltpu.VMEM((PADDED_SPEC, LANES), F32),
            pltpu.VMEM((2, COMPS, LOCAL, LANES), F32),
            dma((6,)),
            dma((4,)),
            dma((4,)),
            dma((2,)),
            dma((2, COMPS)),
            dma((2, COMPS)),
            dma((2,)),
        ],
        compiler_params=pltpu.CompilerParams(
            collective_id=0, has_side_effects=True, vmem_limit_bytes=56 * 1024 * 1024
        ),
        cost_estimate=pl.CostEstimate(flops=2 * SPEC * SPEC * 256, bytes_accessed=16 << 20, transcendentals=0),
        name="exchange",
    )(spectrum.reshape(LOCAL * ROWS, LANES), wind.reshape(2 * ROWS, LANES), sea_table, transfer_kernel, table)
    result = pl.pallas_call(
        expand_kernel,
        out_shape=shape((LOCAL * ROWS, LANES), F32),
        in_specs=[vmem, vmem, vmem, pl.BlockSpec(memory_space=pltpu.SMEM)],
        out_specs=anywhere,
        scratch_shapes=[pltpu.VMEM((PADDED_COMP * ROWS, LANES), F32), dma],
        compiler_params=pltpu.CompilerParams(vmem_limit_bytes=32 * 1024 * 1024),
        cost_estimate=pl.CostEstimate(flops=1 << 20, bytes_accessed=6 << 20, transcendentals=0),
        name="expand",
    )(compact, lane_map, part_map, unit_rows)
    return result.reshape(LOCAL, ROWS, LANES)


def solution(mesh):
    placed = (P("comp", "region", None), P(None, "region", None), P("region", None), P())
    return jax.shard_map(
        on_device, mesh=mesh, in_specs=placed, out_specs=P("comp", "region", None), check_vma=False
    )
```

time: 406 us -> 129 us (0.32); the launches traced: 399 us -> 128 us
  other arithmetic: 127 us -> 0 us
  Pallas kernels: 0 us -> 124 us
  waiting for transfers between devices: 98.5 us -> 0 us
  blocking collectives: 88.3 us -> 0 us
  local copies, waits for them, and re-layouts: 50.7 us -> 4.07 us
  starting transfers between devices: 25 us -> 0 us
  matrix products: 6.86 us -> 0 us
    pallas_call x0 -> x2, Pallas kernels: none -> 124 us  [the longest x1 111 us: on_device(): pl.pallas_call(exchange_kernel, out_shape=(shape((UNITS, LOCAL, LANES), F...]
    all_to_all x1 -> x0, waiting for transfers between devices: 92.3 us -> none  [on_device(): lax.all_to_all(wave_field, 'comp', split_axis=1, concat_axis=0, tiled=True)]
    all_to_all x1 -> x0, blocking collectives: 88.3 us -> none  [on_device(): lax.all_to_all(updated, 'comp', split_axis=0, concat_axis=1, tiled=True)]
    sub x64 -> x0, other arithmetic: 82.2 us -> none  [one_block(): matches = (listed - block_base)[:, None, None] == cell_grid[None]]
    dynamic_slice x64 -> x0, local copies, waits for them, and re-layouts: 37.1 us -> none  [block_marks(): present, slot = lax.map(one_block, (sea_rows, bases))]
    mul x7 -> x0, other arithmetic: 20.4 us -> none  [the longest x2 16.3 us: upwind(): return sea_mask * changed]
    all_to_all x1 -> x0, starting transfers between devices: 15.4 us -> none  [on_device(): lax.all_to_all(wave_field, 'comp', split_axis=1, concat_axis=0, tiled=True)]
    reduce_or x64 -> x0, other arithmetic: 14 us -> none  [one_block(): present = jnp.any(matches, axis=0)]
  transfers between devices with their start and end apart: 5 -> 0, of which waited for: 3 -> 0; matrix products, arithmetic and copies ran while one was open for 0% -> 0% of each run, Pallas kernels for 0% -> 0%
where the time goes in v1:
time: 129 us; the launch traced here: 128 us
  Pallas kernels  124 us (96%)
  local copies, waits for them, and re-layouts  4.07 us (3%)
    pallas_call x1, Pallas kernels, on_device(): pl.pallas_call(exchange_kernel, out_shape=(shape((UNITS, LOCAL, LANES), F...  111 us
    pallas_call x1, Pallas kernels, on_device(): pl.pallas_call(expand_kernel, out_shape=shape((LOCAL * ROWS, LANES), F32)...  13.8 us
    unnamed x8, local copies, waits for them, and re-layouts  4.07 us

profile of v1, /device:TPU:1, one launch (start us, length us, event | category | flops | bytes accessed | tf_op | source)
XLA Modules:
  0.0 128.4 jit_solution(13126459013609226563)
XLA Ops:
  0.0 110.6 %exchange.1 = (f32[128,27,128]{2,1,0:T(8,128)}, s32[264,128]{1,0:T(8,128)}, s32[264,128]{1,0:T(8,128)}, s32[8,128]{1,0:T(8,128)}) custom-call(f32[6912,128]{1,0:T(8,128)} %bitcast.3, f32[512,128]{1,0:T(8,128)} %bitcast.4, s32[64,512]{1,0:T(8,128)} %sea_table.1, bf16[1728,1728]{1,0:T(8,128)(2,1)} %transfer.1, f32[64,27,128]{2,1,0:T(8,128)} %constant.2.clone.table), custom_call_target="tpu_custom_call" | custom-call | flops 1528823808 | bytes 16777216 | tf_op jit(solution)/shard_map/exchange/pallas_call | solution.py:362
  110.6 0.0 copy-start
  110.6 1.6 %copy-done = f32[128,27,128]{2,1,0:T(8,128)S(1)} copy-done((f32[128,27,128]{2,1,0:T(8,128)S(1)}, f32[128,27,128]{2,1,0:T(8,128)}, u32[]{:S(2)}) %copy-start) | copy-done | bytes 1769496
  112.2 0.0 copy-start.1
  112.2 0.9 copy-done.1
  113.1 0.0 copy-start.2
  113.1 0.9 copy-done.2
  114.0 0.0 copy-start.3
  114.0 0.7 copy-done.3
  114.7 13.8 %expand.1 = f32[6912,128]{1,0:T(8,128)} custom-call(f32[128,27,128]{2,1,0:T(8,128)S(1)} %copy-done, s32[264,128]{1,0:T(8,128)S(1)} %copy-done.1, s32[264,128]{1,0:T(8,128)S(1)} %copy-done.2, s32[8,128]{1,0:T(8,128)S(1)} %copy-done.3), custom_call_target="tpu_custom_call" | custom-call | flops 1048576 | bytes 6291456 | tf_op jit(solution)/shard_map/expand/pallas_call | solution.py:407
Async XLA Ops:
  110.6 1.6 %copy-start = (f32[128,27,128]{2,1,0:T(8,128)S(1)}, f32[128,27,128]{2,1,0:T(8,128)}, u32[]{:S(2)}) copy-start(f32[128,27,128]{2,1,0:T(8,128)} %get-tuple-element.9.compact) | copy-start | bytes 5308420
  112.2 0.9 copy-start.1
  113.1 0.9 copy-start.2
  114.0 0.7 copy-start.3

commit v2 on v1

v2 whole, which is shorter than its diff:
```python
import math

import jax
import jax.numpy as jnp
import numpy as np
from jax import lax
from jax.experimental import pallas as pl
from jax.experimental.pallas import tpu as pltpu
from jax.sharding import PartitionSpec as P

NDIR = 36
NFREQ = 48
SPEC = NDIR * NFREQ
COMPS = 64
LOCAL = SPEC // COMPS
REGIONS = 4
ROWS = 256
LANES = 128
BLOCKS = 64
STRIDE = ROWS + 16
PADDED_ROWS = ROWS + 8
PADDED_COMP = 32
PADDED_SPEC = SPEC + 32
TILE = 432
F32 = jnp.float32
MESH = pl.DeviceIdType.MESH

growth_rate = 0.05
wind_floor = 0.5
dissipation = 0.02
coupling = 0.5
courant_top = 0.6


def component_tables():
    comp = np.arange(SPEC)
    freq, direction = comp // NDIR, 2.0 * math.pi * (comp % NDIR + 0.5) / NDIR
    omega = 1.1 ** (freq - NFREQ // 2)
    speed = courant_top * 1.1 ** (-freq.astype(np.float64))
    cosine, sine = np.cos(direction), np.sin(direction)
    u, v = speed * cosine, speed * sine
    centre = 1.0 - np.abs(u) - np.abs(v)
    columns = [omega, cosine, sine, centre, np.maximum(u, 0), np.maximum(-u, 0), np.maximum(v, 0), np.maximum(-v, 0)]
    table = np.zeros((SPEC, LANES), np.float32)
    for lane, column in enumerate(columns):
        table[:, lane] = column
    scalars = np.zeros((COMPS, 8, LANES), np.float32)
    for row, column in enumerate([centre, np.abs(u), np.abs(v)]):
        scalars[:, row, :LOCAL] = column.reshape(COMPS, LOCAL)
    return table.reshape(COMPS, LOCAL, LANES), scalars


def energy_scale():
    return float(1.0 / (NDIR * np.sum(1.1 ** (np.arange(NFREQ) - NFREQ // 2.0))))


def shifted(me, step):
    z = (me // 8 + step // 8) % 8
    y = ((me // 2) % 4 + (step // 2) % 4) % 4
    core = (me % 2 + step % 2) % 2
    return z * 8 + y * 2 + core


def gathered(source, lanes):
    return jnp.take_along_axis(source, lanes, axis=1, mode="promise_in_bounds")


def spread_rows(row):
    return jnp.broadcast_to(row, (LOCAL, LANES))


def exchange_kernel(
    spectrum, wind_field, sea_table, transfer, table, scalars,
    result,
    wave0, wave1, mask, sea_rows, lane_map, part_map, units, units_smem, scalars_smem,
    wind, kernel_buf, constants, own, omega, cosine, sine,
    to_west, to_east, from_west, from_east,
    outgoing, incoming, dense, rounded, coupled, returning, arrived_a, arrived_b, expanded, spread,
    load_sem, comp_sem, halo_send, halo_recv, send_sem, forward_sem, back_sem, store_sem,
):
    me = lax.axis_index("comp")
    region = lax.axis_index("region")
    west = (region + REGIONS - 1) % REGIONS
    east = (region + 1) % REGIONS

    def comp_load(comp):
        return pltpu.make_async_copy(
            spectrum.at[comp], wave0.at[pl.ds(pl.multiple_of(comp * STRIDE + 8, 8), ROWS)], comp_sem.at[comp])

    load_scalars = pltpu.make_async_copy(scalars.at[me], scalars_smem, load_sem.at[0])
    load_scalars.start()
    load_own = pltpu.make_async_copy(table.at[me], own, load_sem.at[1])
    load_own.start()

    @pl.loop(0, LOCAL)
    def _(comp):
        comp_load(comp).start()

    barrier = pltpu.get_barrier_semaphore()

    @pl.loop(1, COMPS)
    def _(step):
        pl.semaphore_signal(barrier, inc=1, device_id={"comp": shifted(me, step)}, device_id_type=MESH)

    pl.semaphore_signal(barrier, inc=1, device_id={"region": west}, device_id_type=MESH)
    pl.semaphore_signal(barrier, inc=1, device_id={"region": east}, device_id_type=MESH)

    load_constants = pltpu.make_async_copy(table, constants, load_sem.at[2])
    load_constants.start()
    load_kernel = pltpu.make_async_copy(transfer, kernel_buf, load_sem.at[3])
    load_kernel.start()
    load_wind = pltpu.make_async_copy(wind_field, wind.at[pl.ds(0, 2 * ROWS)], load_sem.at[4])
    load_wind.start()

    for part in range(4):
        sea_rows[pl.ds(part, BLOCKS, stride=4), :] = sea_table[:, part * LANES : (part + 1) * LANES]

    row_number = lax.broadcasted_iota(jnp.int32, (ROWS, LANES), 0)
    lane_position = lax.broadcasted_iota(jnp.int32, (ROWS, LANES), 1)
    later = (sea_rows[0:ROWS, :] >= 0) & ((row_number & 3) > 0)
    count = jnp.where(later, 1.0, 0.0)
    lower = jnp.where(
        lax.broadcasted_iota(jnp.int32, (ROWS, ROWS), 0) > lax.broadcasted_iota(jnp.int32, (ROWS, ROWS), 1), 1.0, 0.0
    ).astype(jnp.bfloat16)
    rank = jnp.dot(lower, count.astype(jnp.bfloat16), preferred_element_type=F32)
    found = jnp.where((rank == lane_position.astype(F32)) & later, row_number.astype(F32), 0.0)
    before = jnp.where(row_number < lane_position * 4, count, 0.0)
    unit_rows = jnp.broadcast_to(jnp.sum(found, axis=0, keepdims=True), (4, LANES))
    first_units = jnp.broadcast_to(jnp.sum(before, axis=0, keepdims=True), (4, LANES))
    units[...] = jnp.concatenate([unit_rows, first_units], axis=0).astype(jnp.int32)
    load_units = pltpu.make_async_copy(units, units_smem, load_sem.at[5])
    load_units.start()

    lane_number = lax.broadcasted_iota(jnp.int32, (LANES, 4 * LANES), 0)
    quarter = lax.broadcasted_iota(jnp.int32, (8, 4 * LANES), 0)

    def listed_maps(block, weights):
        cells = sea_table[pl.ds(block, 1), :]
        lane = jnp.where(cells >= 0, cells & (LANES - 1), -1)
        inside = jnp.where(cells >= 0, (cells >> 7) & 3, -1)
        match = jnp.where(lane == lane_number, 1.0, 0.0).astype(jnp.bfloat16)
        row = jnp.where(inside == quarter, 1.0, 0.0)
        rows = jnp.concatenate([row * w for w in weights], axis=0).astype(jnp.bfloat16)
        return lax.dot_general(rows, match, (((1,), (1,)), ((), ())), preferred_element_type=F32)

    def block_rows(block):
        return pl.ds(pl.multiple_of(block * 4, 4), 4)

    @pl.loop(0, BLOCKS, unroll=8)
    def _(block):
        mask[block_rows(block), :] = listed_maps(block, [1.0])[0:4]

    def strided(x):
        return pl.ds(x, LOCAL, stride=STRIDE)

    @pl.loop(0, LOCAL)
    def _(comp):
        comp_load(comp).wait()
        base = pl.multiple_of(comp * STRIDE + 8, 8)
        for start in range(0, ROWS, 64):
            rows = pl.ds(base + start, 64)
            wave0[rows, :] = mask[start : start + 64, :] * wave0[rows, :]

    first_row, last_row = wave0[strided(8), :], wave0[strided(7 + ROWS), :]
    to_west[0] = first_row
    to_west[1] = wave0[strided(9), :]
    to_west[2] = spread_rows(mask[0:1, :])
    to_east[0] = last_row
    to_east[1] = wave0[strided(6 + ROWS), :]
    to_east[2] = spread_rows(mask[ROWS - 1 : ROWS, :])
    pl.semaphore_wait(barrier, COMPS + 1)
    send_west = pltpu.make_async_remote_copy(
        to_west, from_east, halo_send.at[0], halo_recv.at[0], device_id={"region": west}, device_id_type=MESH)
    send_east = pltpu.make_async_remote_copy(
        to_east, from_west, halo_send.at[1], halo_recv.at[1], device_id={"region": east}, device_id_type=MESH)
    send_west.start()
    send_east.start()

    load_scalars.wait()
    lanes = lax.broadcasted_iota(jnp.int32, (8, LANES), 1)

    def substep(source, target, groups):
        @pl.loop(0, LOCAL)
        def _(comp):
            direction = (me * LOCAL + comp) % NDIR
            aside = jnp.where((direction < NDIR // 4) | (direction >= 3 * NDIR // 4), -1, 1)
            turn = jnp.where(direction < NDIR // 2, 1, LANES - 1)
            edge = jnp.where(direction < NDIR // 2, 0, LANES - 1)
            centre_w = jnp.full((8, LANES), scalars_smem[0, comp])
            x_w = jnp.full((8, LANES), scalars_smem[1, comp])
            y_w = jnp.where(lanes == edge, 0.0, scalars_smem[2, comp])
            base = pl.multiple_of(comp * STRIDE + 8, 8)
            for group in groups:
                here = source[pl.ds(base + 8 * group, 8), :]
                beside = source[pl.ds(base + 8 * group + aside, 8), :]
                changed = centre_w * here + x_w * beside + y_w * pltpu.roll(here, turn, 1)
                target[pl.ds(base + 8 * group, 8), :] = mask[8 * group : 8 * group + 8, :] * changed

    substep(wave0, wave1, range(1, ROWS // 8 - 1))

    load_own.wait()
    coefficients = own[...]
    wide = lax.broadcasted_iota(jnp.int32, (LOCAL, LANES), 1)

    def column(number):
        return spread_rows(coefficients[:, number : number + 1])

    centre_w, west_w, east_w = column(3), column(4), column(5)
    south_w = jnp.where(wide == 0, 0.0, column(6))
    north_w = jnp.where(wide == LANES - 1, 0.0, column(7))

    def halo(rows, inside, outermost, before):
        near = jnp.where(inside, rows[0], 0.0)
        far = jnp.where(inside, rows[1], 0.0)
        sides = (far, outermost) if before else (outermost, far)
        changed = (
            centre_w * near + west_w * sides[0] + east_w * sides[1]
            + south_w * pltpu.roll(near, 1, 1) + north_w * pltpu.roll(near, LANES - 1, 1)
        )
        at = strided(7 if before else 8 + ROWS)
        wave0[at, :] = near
        wave1[at, :] = rows[2] * changed

    send_west.wait()
    send_east.wait()
    halo(from_west, region > 0, first_row, True)
    halo(from_east, region < REGIONS - 1, last_row, False)
    substep(wave0, wave1, (0, ROWS // 8 - 1))
    substep(wave1, wave0, range(ROWS // 8))

    load_units.wait()

    def packed(row):
        cells = sea_rows[pl.ds(row, 1), :]
        base = row & ~3
        lane = spread_rows(cells & (LANES - 1))
        inside = spread_rows((cells >> 7) & 3)
        total = gathered(wave0[strided(8 + base), :], lane)
        for number in range(1, 4):
            total = jnp.where(inside == number, gathered(wave0[strided(8 + base + number), :], lane), total)
        return total

    def unit_row(chunk, device):
        return jnp.clip(units_smem[0, device], 0, ROWS - 1) if chunk == 0 else device * 4

    def forward(chunk, target):
        return pltpu.make_async_remote_copy(
            outgoing.at[chunk, target], incoming.at[chunk, me], send_sem.at[chunk], forward_sem.at[chunk, me],
            device_id={"comp": target}, device_id_type=MESH)

    for chunk in range(2):

        @pl.loop(1, COMPS)
        def _(step, chunk=chunk):
            target = shifted(me, step)
            outgoing[chunk, target] = packed(unit_row(chunk, target))
            forward(chunk, target).start()

    for chunk in range(2):
        incoming[chunk, me] = packed(unit_row(chunk, me))

    load_constants.wait()

    @pl.loop(0, COMPS, unroll=4)
    def _(source):
        values = constants[source]
        omega[source] = spread_rows(values[:, 0:1])
        cosine[source] = spread_rows(values[:, 1:2])
        sine[source] = spread_rows(values[:, 2:3])

    slot = lax.broadcasted_iota(jnp.int32, (1, 4 * LANES), 1)
    slot_lane = (slot & (LANES - 1)).astype(F32)
    slot_part = (slot >> 7).astype(F32)

    @pl.loop(0, BLOCKS, unroll=8)
    def _(block):
        maps = listed_maps(block, [slot_lane, slot_part])
        rows = block_rows(block)
        lane_map[rows, :] = maps[0:4].astype(jnp.int32)
        part_map[rows, :] = jnp.where(mask[rows, :] > 0.5, maps[8:12], -1.0).astype(jnp.int32)

    load_kernel.wait()
    load_wind.wait()

    def wind_at(row):
        cells = sea_rows[pl.ds(row, 1), :]
        base = row & ~3
        lane = jnp.broadcast_to(cells & (LANES - 1), (8, LANES))
        inside = (cells >> 7) & 3
        parts = []
        for part in range(2):
            total = jnp.zeros((8, LANES), F32)
            for number in range(4):
                line = jnp.broadcast_to(wind[pl.ds(part * ROWS + base + number, 1), :], (8, LANES))
                total = jnp.where(inside == number, gathered(line, lane), total)
            parts.append(total[0:1])
        return parts

    def back(chunk, target, held):
        return pltpu.make_async_remote_copy(
            returning.at[chunk, target], held.at[me], send_sem.at[2 + chunk], back_sem.at[chunk, me],
            device_id={"comp": target}, device_id_type=MESH)

    for chunk, held in enumerate((arrived_a, arrived_b)):

        @pl.loop(1, COMPS)
        def _(step, chunk=chunk):
            source = shifted(me, step)
            pltpu.make_async_remote_copy(
                outgoing.at[chunk, source], incoming.at[chunk, source], send_sem.at[chunk], forward_sem.at[chunk, source],
                device_id={"comp": source}, device_id_type=MESH).wait_recv()

        wind_u, wind_v = wind_at(unit_row(chunk, me))

        def collect(source, total, chunk=chunk):
            values = incoming[chunk, source]
            dense[pl.ds(source * LOCAL, LOCAL), :] = values
            return total + omega[source] * values

        total = lax.fori_loop(0, COMPS, collect, jnp.zeros((LOCAL, LANES), F32), unroll=True)
        energy = jnp.sum(total, axis=0, keepdims=True) * energy_scale()
        loss = dissipation * energy * energy
        rounded[...] = dense[0:SPEC, :].astype(jnp.bfloat16)

        @pl.loop(0, SPEC // TILE)
        def _(tile):
            rows = pl.ds(pl.multiple_of(tile * TILE, TILE), TILE)
            coupled[rows, :] = jnp.dot(kernel_buf[rows, :], rounded[...], preferred_element_type=F32)

        def updated(target, chunk=chunk, wind_u=wind_u, wind_v=wind_v, loss=loss):
            points = incoming[chunk, target]
            speed = omega[target]
            along = cosine[target] * wind_u + sine[target] * wind_v
            growth = growth_rate * speed * jnp.maximum(along - wind_floor, 0.0)
            damping = speed * speed * loss
            joined = coupled[pl.ds(target * LOCAL, LOCAL), :]
            return points + points * (growth - damping + coupling * joined) / (1.0 + damping)

        @pl.loop(1, COMPS)
        def _(step, chunk=chunk, held=held, updated=updated):
            target = shifted(me, step)
            returning[chunk, target] = updated(target)
            back(chunk, target, held).start()

        held[me] = updated(me)

    def wait_back(chunk, source, held):
        pltpu.make_async_remote_copy(
            returning.at[chunk, source], held.at[source], send_sem.at[2 + chunk], back_sem.at[chunk, source],
            device_id={"comp": source}, device_id_type=MESH).wait_recv()

    @pl.loop(1, COMPS)
    def _(step):
        wait_back(0, shifted(me, step), arrived_a)

    @pl.loop(0, BLOCKS)
    def _(block):
        first_unit = units_smem[4, block]
        pieces = []
        for number in range(4):
            line = pl.ds(block * 4 + number, 1)
            lane, part = spread_rows(lane_map[line, :]), spread_rows(part_map[line, :])
            total = jnp.zeros((LOCAL, LANES), F32)
            for offset in range(3):
                values = arrived_a[jnp.clip(first_unit + offset, 0, COMPS - 1)]
                total = jnp.where(part == offset + 1, gathered(values, lane), total)
            pieces.append(total)
        for number in range(4):
            expanded[block * 4 + number] = pieces[number]

    def store(chip):
        return pltpu.make_async_copy(
            spread.at[chip, pl.ds(0, LOCAL * 8)].reshape(LOCAL, 8, LANES),
            result.at[:, pl.ds(pl.multiple_of(chip * 8, 8), 8), :], store_sem.at[0])

    def finish(chip):
        pieces = []
        for core in range(2):
            values = arrived_b[2 * chip + core]
            for number in range(4):
                x = chip * 8 + core * 4 + number
                line = pl.ds(x, 1)
                lane, part = spread_rows(lane_map[line, :]), spread_rows(part_map[line, :])
                pieces.append(jnp.where(part == 0, gathered(values, lane), expanded[x]))
        for number, piece in enumerate(pieces):
            spread[chip, pl.ds(number, LOCAL, stride=8), :] = piece
        store(chip).start()

    wait_back(1, shifted(me, 1), arrived_b)
    finish(me // 2)

    @pl.loop(1, COMPS // 2)
    def _(step):
        chip = (me // 8 + 8 - step // 4) % 8 * 4 + ((me // 2) % 4 + 4 - step % 4) % 4
        wait_back(1, 2 * chip, arrived_b)
        wait_back(1, 2 * chip + 1, arrived_b)
        finish(chip)

    for number in range(4):
        sent = outgoing.at[0, pl.ds(0, COMPS - 1)]
        pltpu.make_async_copy(sent, sent, send_sem.at[number]).wait()
    pltpu.make_async_copy(result, result, store_sem.at[0]).wait()


def on_device(spectrum, wind, sea_table, transfer_kernel):
    table, scalars = (jnp.asarray(array) for array in component_tables())
    vmem = pl.BlockSpec(memory_space=pltpu.VMEM)
    anywhere = pl.BlockSpec(memory_space=pl.ANY)
    wave = pltpu.VMEM((PADDED_COMP * STRIDE, LANES), F32)
    line_map = pltpu.VMEM((PADDED_ROWS, LANES), jnp.int32)
    per_source = pltpu.VMEM((COMPS, LOCAL, LANES), F32)
    per_chunk = pltpu.VMEM((2, COMPS, LOCAL, LANES), F32)
    rim = pltpu.VMEM((3, LOCAL, LANES), F32)
    dense = pltpu.VMEM((PADDED_SPEC, LANES), F32)
    dma = pltpu.SemaphoreType.DMA
    return pl.pallas_call(
        exchange_kernel,
        out_shape=jax.ShapeDtypeStruct((LOCAL, ROWS, LANES), F32),
        in_specs=[anywhere, anywhere, vmem, anywhere, anywhere, anywhere],
        out_specs=anywhere,
        scratch_shapes=[
            wave,
            wave,
            pltpu.VMEM((PADDED_ROWS, LANES), F32),
            line_map,
            line_map,
            line_map,
            pltpu.VMEM((8, LANES), jnp.int32),
            pltpu.SMEM((8, LANES), jnp.int32),
            pltpu.SMEM((8, LANES), F32),
            pltpu.VMEM((2 * ROWS + 8, LANES), F32),
            pltpu.VMEM((SPEC, SPEC), jnp.bfloat16),
            per_source,
            pltpu.VMEM((LOCAL, LANES), F32),
            per_source,
            per_source,
            per_source,
            rim,
            rim,
            rim,
            rim,
            per_chunk,
            per_chunk,
            dense,
            pltpu.VMEM((SPEC, LANES), jnp.bfloat16),
            dense,
            per_chunk,
            per_source,
            per_source,
            pltpu.VMEM((ROWS, LOCAL, LANES), F32),
            pltpu.VMEM((COMPS // 2, 256, LANES), F32),
            dma((6,)),
            dma((LOCAL,)),
            dma((2,)),
            dma((2,)),
            dma((4,)),
            dma((2, COMPS)),
            dma((2, COMPS)),
            dma((1,)),
        ],
        compiler_params=pltpu.CompilerParams(
            collective_id=0, has_side_effects=True, vmem_limit_bytes=56 * 1024 * 1024
        ),
        cost_estimate=pl.CostEstimate(flops=2 * SPEC * SPEC * 256, bytes_accessed=16 << 20, transcendentals=0),
        name="exchange",
    )(spectrum, wind.reshape(2 * ROWS, LANES), sea_table, transfer_kernel, table, scalars)


def solution(mesh):
    placed = (P("comp", "region", None), P(None, "region", None), P("region", None), P())
    return jax.shard_map(
        on_device, mesh=mesh, in_specs=placed, out_specs=P("comp", "region", None), check_vma=False
    )
```

time: 129 us -> 113 us (0.88)
  Pallas kernels: 124 us -> 108 us
    pallas_call x2 -> x1, Pallas kernels: 124 us -> 108 us  [on_device(): pl.pallas_call(exchange_kernel, out_shape=jax.ShapeDtypeStruct((LOCAL, RO...]
    unnamed x8 -> x1, local copies, waits for them, and re-layouts: 4.07 us -> 4.17 us
where the time goes in v2:
time: 113 us; the launch traced here: 112 us
  Pallas kernels  108 us (96%)
  local copies, waits for them, and re-layouts  4.17 us (4%)
    pallas_call x1, Pallas kernels, on_device(): pl.pallas_call(exchange_kernel, out_shape=jax.ShapeDtypeStruct((LOCAL, RO...  108 us
    unnamed x1, local copies, waits for them, and re-layouts  4.17 us

profile of v2, /device:TPU:1, one launch (start us, length us, event | category | flops | bytes accessed | tf_op | source)
XLA Modules:
  0.0 112.5 jit_solution(7547009899443727431)
XLA Ops:
  0.0 108.3 %exchange.1 = f32[27,256,128]{2,1,0:T(8,128)} custom-call(f32[27,256,128]{2,1,0:T(8,128)} %spectrum.1, f32[512,128]{1,0:T(8,128)} %bitcast.1, s32[64,512]{1,0:T(8,128)} %sea_table.1, bf16[1728,1728]{1,0:T(8,128)(2,1)} %transfer.1, f32[64,27,128]{2,1,0:T(8,128)} %constant.4.clone.table, f32[64,8,128]{2,1,0:T(8,128)} %constant.5.clone.scalars), custom_call_target="tpu_custom_call" | custom-call | flops 1528823808 | bytes 16777216 | tf_op jit(solution)/shard_map/exchange/pallas_call | solution.py:416
  108.3 4.2 %copy.8 = f32[27,256,128]{2,1,0:T(8,128)} copy(f32[27,256,128]{2,1,0:T(8,128)} %exchange.1) | data formatting | bytes 7077888

commit v3 on v2

v3 whole, which is shorter than its diff:
```python
import math

import jax
import jax.numpy as jnp
import numpy as np
from jax import lax
from jax.experimental import pallas as pl
from jax.experimental.pallas import tpu as pltpu
from jax.sharding import PartitionSpec as P

NDIR = 36
NFREQ = 48
SPEC = NDIR * NFREQ
COMPS = 64
LOCAL = SPEC // COMPS
REGIONS = 4
ROWS = 256
LANES = 128
BLOCKS = 64
STRIDE = ROWS + 16
PADDED_ROWS = ROWS + 8
PADDED_COMP = 32
PADDED_SPEC = SPEC + 32
TILE = 432
EARLY = 20
SHARE = 9
F32 = jnp.float32
MESH = pl.DeviceIdType.MESH

growth_rate = 0.05
wind_floor = 0.5
dissipation = 0.02
coupling = 0.5
courant_top = 0.6


def component_tables():
    comp = np.arange(SPEC)
    freq, direction = comp // NDIR, 2.0 * math.pi * (comp % NDIR + 0.5) / NDIR
    omega = 1.1 ** (freq - NFREQ // 2)
    speed = courant_top * 1.1 ** (-freq.astype(np.float64))
    cosine, sine = np.cos(direction), np.sin(direction)
    u, v = speed * cosine, speed * sine
    centre = 1.0 - np.abs(u) - np.abs(v)
    columns = [omega, cosine, sine, centre, np.maximum(u, 0), np.maximum(-u, 0), np.maximum(v, 0), np.maximum(-v, 0)]
    table = np.zeros((SPEC, LANES), np.float32)
    for lane, column in enumerate(columns):
        table[:, lane] = column
    scalars = np.zeros((COMPS, 8, LANES), np.float32)
    for row, column in enumerate([centre, np.abs(u), np.abs(v)]):
        scalars[:, row, :LOCAL] = column.reshape(COMPS, LOCAL)
    return table.reshape(COMPS, LOCAL, LANES), scalars


def energy_scale():
    return float(1.0 / (NDIR * np.sum(1.1 ** (np.arange(NFREQ) - NFREQ // 2.0))))


def shifted(me, step):
    z = ((me & 56) + (step & 56)) & 56
    y = ((me & 6) + (step & 6)) & 6
    return z + y + ((me + step) & 1)


def gathered(source, lanes):
    return jnp.take_along_axis(source, lanes, axis=1, mode="promise_in_bounds")


def spread_rows(row):
    return jnp.broadcast_to(row, (LOCAL, LANES))


def exchange_kernel(
    spectrum, wind_field, listed, transfer, table, scalars,
    result,
    wave0, wave1, wave2, sea_table, mask, sea_rows, lane_map, part_map, units, units_smem, scalars_smem,
    wind, kernel_buf, constants, own, omega, cosine, sine,
    to_west, to_east, from_west, from_east,
    outgoing, incoming, dense, rounded, coupled, returning, arrived_a, arrived_b, expanded,
    load_sem, comp_sem, halo_send, halo_recv, send_sem, forward_sem, back_sem,
):
    me = lax.axis_index("comp")
    region = lax.axis_index("region")
    west = (region + REGIONS - 1) & (REGIONS - 1)
    east = (region + 1) & (REGIONS - 1)

    def comp_load(comp):
        return pltpu.make_async_copy(
            spectrum.at[comp], wave0.at[pl.ds(comp * STRIDE + 8, ROWS)], comp_sem.at[comp // SHARE])

    barrier = pltpu.get_barrier_semaphore()

    for step in range(1, COMPS):
        pl.semaphore_signal(barrier, inc=1, device_id={"comp": shifted(me, step)}, device_id_type=MESH)
    pl.semaphore_signal(barrier, inc=1, device_id={"region": west}, device_id_type=MESH)
    pl.semaphore_signal(barrier, inc=1, device_id={"region": east}, device_id_type=MESH)

    load_listed = pltpu.make_async_copy(listed, sea_table, load_sem.at[6])
    load_listed.start()

    for comp in range(LOCAL):
        comp_load(comp).start()

    load_scalars = pltpu.make_async_copy(scalars.at[me], scalars_smem, load_sem.at[0])
    load_scalars.start()
    load_own = pltpu.make_async_copy(table.at[me], own, load_sem.at[1])
    load_own.start()
    load_constants = pltpu.make_async_copy(table, constants, load_sem.at[2])
    load_kernel = pltpu.make_async_copy(transfer, kernel_buf, load_sem.at[3])
    load_wind = pltpu.make_async_copy(wind_field, wind.at[pl.ds(0, 2 * ROWS)], load_sem.at[4])
    load_listed.wait()

    for part in range(4):
        sea_rows[pl.ds(part, BLOCKS, stride=4), :] = sea_table[:, part * LANES : (part + 1) * LANES]

    lane_number = lax.broadcasted_iota(jnp.int32, (LANES, 4 * LANES), 0)
    quarter = lax.broadcasted_iota(jnp.int32, (8, 4 * LANES), 0)

    def listed_maps(block, weights):
        cells = sea_table[pl.ds(block, 1), :]
        lane = jnp.where(cells >= 0, cells & (LANES - 1), -1)
        inside = jnp.where(cells >= 0, (cells >> 7) & 3, -1)
        match = jnp.where(lane == lane_number, 1.0, 0.0).astype(jnp.bfloat16)
        row = jnp.where(inside == quarter, 1.0, 0.0)
        rows = jnp.concatenate([row * w for w in weights], axis=0).astype(jnp.bfloat16)
        return lax.dot_general(rows, match, (((1,), (1,)), ((), ())), preferred_element_type=F32)

    def block_rows(block):
        return pl.ds(pl.multiple_of(block * 4, 4), 4)

    @pl.loop(0, BLOCKS, unroll=8)
    def _(block):
        mask[block_rows(block), :] = listed_maps(block, [1.0])[0:4]

    def strided(x):
        return pl.ds(x, LOCAL, stride=STRIDE)

    for share in range(LOCAL // SHARE):
        landed = wave0.at[pl.ds(0, SHARE * ROWS)]
        pltpu.make_async_copy(landed, landed, comp_sem.at[share]).wait()

        @pl.loop(share * SHARE, (share + 1) * SHARE)
        def _(comp):
            base = pl.multiple_of(comp * STRIDE + 8, 8)
            for start in range(0, ROWS, 64):
                rows = pl.ds(base + start, 64)
                wave0[rows, :] = mask[start : start + 64, :] * wave0[rows, :]

    nothing = jnp.zeros((LOCAL, LANES), F32)
    for wave in (wave0, wave1):
        wave[strided(7), :] = nothing
        wave[strided(8 + ROWS), :] = nothing

    first_row, last_row = wave0[strided(8), :], wave0[strided(7 + ROWS), :]
    to_west[0] = first_row
    to_west[1] = wave0[strided(9), :]
    to_west[2] = spread_rows(mask[0:1, :])
    to_east[0] = last_row
    to_east[1] = wave0[strided(6 + ROWS), :]
    to_east[2] = spread_rows(mask[ROWS - 1 : ROWS, :])
    pl.semaphore_wait(barrier, COMPS + 1)
    send_west = pltpu.make_async_remote_copy(
        to_west, from_east, halo_send.at[0], halo_recv.at[0], device_id={"region": west}, device_id_type=MESH)
    send_east = pltpu.make_async_remote_copy(
        to_east, from_west, halo_send.at[1], halo_recv.at[1], device_id={"region": east}, device_id_type=MESH)
    send_west.start()
    send_east.start()

    load_scalars.wait()
    lanes = lax.broadcasted_iota(jnp.int32, (8, LANES), 1)

    def substep(source, target, groups, unroll, origin=0):
        @pl.loop(0, LOCAL, unroll=unroll)
        def _(comp):
            direction = lax.rem(me * LOCAL + comp, NDIR)
            aside = jnp.where((direction < NDIR // 4) | (direction >= 3 * NDIR // 4), -1, 1)
            turn = jnp.where(direction < NDIR // 2, 1, LANES - 1)
            edge = jnp.where(direction < NDIR // 2, 0, LANES - 1)
            centre_w = jnp.full((8, LANES), scalars_smem[0, comp])
            x_w = jnp.full((8, LANES), scalars_smem[1, comp])
            y_w = jnp.where(lanes == edge, 0.0, scalars_smem[2, comp])
            for group in groups:
                row = pl.multiple_of(origin + 8 * group, 8)
                base = pl.multiple_of(comp * STRIDE + 8 + row, 8)
                here = source[pl.ds(base, 8), :]
                beside = source[pl.ds(base + aside, 8), :]
                changed = centre_w * here + x_w * beside + y_w * pltpu.roll(here, turn, 1)
                target[pl.ds(base, 8), :] = mask[pl.ds(row, 8), :] * changed

    substep(wave0, wave1, range(ROWS // 8), 3)

    def packed(row):
        cells = sea_rows[pl.ds(row, 1), :]
        base = row & ~3
        lane = spread_rows(cells & (LANES - 1))
        inside = spread_rows((cells >> 7) & 3)
        total = gathered(wave2[strided(8 + base), :], lane)
        for number in range(1, 4):
            total = jnp.where(inside == number, gathered(wave2[strided(8 + base + number), :], lane), total)
        return total

    def unit_row(chunk, device):
        return jnp.clip(units_smem[0, device], 0, ROWS - 1) if chunk == 0 else device * 4

    def forward(chunk, target):
        return pltpu.make_async_remote_copy(
            outgoing.at[chunk, target], incoming.at[chunk, me], send_sem.at[chunk], forward_sem.at[chunk],
            device_id={"comp": target}, device_id_type=MESH)

    def send(chunk, target):
        outgoing[chunk, target] = packed(unit_row(chunk, target))
        forward(chunk, target).start()

    def quarter_sends(number, order):
        part = ((me >> 4) + order) & 3
        substep(wave1, wave2, range(8), 9, origin=part * 64)

        @pl.loop(0, 16)
        def _(place):
            target = part * 16 + ((me + place) & 15)
            ready = (target >= 4) & (target < BLOCKS - 4) if number == 0 else target != me

            @pl.when(ready)
            def _():
                send(1, target)

    quarter_sends(0, 2)
    load_kernel.start()
    load_constants.start()
    load_wind.start()

    load_own.wait()
    coefficients = own[...]
    wide = lax.broadcasted_iota(jnp.int32, (LOCAL, LANES), 1)

    def column(number):
        return spread_rows(coefficients[:, number : number + 1])

    centre_w, west_w, east_w = column(3), column(4), column(5)
    south_w = jnp.where(wide == 0, 0.0, column(6))
    north_w = jnp.where(wide == LANES - 1, 0.0, column(7))

    def halo(rows, inside, outermost, before):
        near = jnp.where(inside, rows[0], 0.0)
        far = jnp.where(inside, rows[1], 0.0)
        sides = (far, outermost) if before else (outermost, far)
        changed = (
            centre_w * near + west_w * sides[0] + east_w * sides[1]
            + south_w * pltpu.roll(near, 1, 1) + north_w * pltpu.roll(near, LANES - 1, 1)
        )
        at = strided(7 if before else 8 + ROWS)
        wave0[at, :] = near
        wave1[at, :] = rows[2] * changed

    send_west.wait()
    send_east.wait()
    halo(from_west, region > 0, first_row, True)
    halo(from_east, region < REGIONS - 1, last_row, False)
    substep(wave0, wave1, (0, ROWS // 8 - 1), 9)
    substep(wave1, wave2, (0, ROWS // 8 - 1), 9)
    quarter_sends(1, 1)

    row_number = lax.broadcasted_iota(jnp.int32, (ROWS, LANES), 0)
    lane_position = lax.broadcasted_iota(jnp.int32, (ROWS, LANES), 1)
    later = (sea_rows[0:ROWS, :] >= 0) & ((row_number & 3) > 0)
    count = jnp.where(later, 1.0, 0.0)
    lower = jnp.where(
        lax.broadcasted_iota(jnp.int32, (ROWS, ROWS), 0) > lax.broadcasted_iota(jnp.int32, (ROWS, ROWS), 1), 1.0, 0.0
    ).astype(jnp.bfloat16)
    rank = jnp.dot(lower, count.astype(jnp.bfloat16), preferred_element_type=F32)
    found = jnp.where((rank == lane_position.astype(F32)) & later, row_number.astype(F32), 0.0)
    before = jnp.where(row_number < lane_position * 4, count, 0.0)
    unit_rows = jnp.broadcast_to(jnp.sum(found, axis=0, keepdims=True), (4, LANES))
    first_units = jnp.broadcast_to(jnp.sum(before, axis=0, keepdims=True), (4, LANES))
    units[...] = jnp.concatenate([unit_rows, first_units], axis=0).astype(jnp.int32)
    load_units = pltpu.make_async_copy(units, units_smem, load_sem.at[5])
    load_units.start()

    quarter_sends(2, 3)
    quarter_sends(3, 0)

    @pl.loop(0, 4)
    def _(place):
        part = ((me >> 4) + 2) & 3

        @pl.when((part == 0) | (part == 3))
        def _():
            send(1, part * 20 + ((me + place) & 3))

    load_units.wait()

    @pl.loop(1, COMPS)
    def _(step):
        send(0, shifted(me, step))

    for chunk in range(2):
        incoming[chunk, me] = packed(unit_row(chunk, me))

    load_constants.wait()

    @pl.loop(0, COMPS, unroll=4)
    def _(source):
        values = constants[source]
        omega[source] = spread_rows(values[:, 0:1])
        cosine[source] = spread_rows(values[:, 1:2])
        sine[source] = spread_rows(values[:, 2:3])

    slot = lax.broadcasted_iota(jnp.int32, (1, 4 * LANES), 1)
    slot_lane = (slot & (LANES - 1)).astype(F32)
    slot_part = (slot >> 7).astype(F32)

    @pl.loop(0, BLOCKS, unroll=8)
    def _(block):
        maps = listed_maps(block, [slot_lane, slot_part])
        rows = block_rows(block)
        lane_map[rows, :] = maps[0:4].astype(jnp.int32)
        part_map[rows, :] = jnp.where(mask[rows, :] > 0.5, maps[8:12], -1.0).astype(jnp.int32)

    load_kernel.wait()
    load_wind.wait()

    def wind_at(row):
        cells = sea_rows[pl.ds(row, 1), :]
        base = row & ~3
        lane = jnp.broadcast_to(cells & (LANES - 1), (8, LANES))
        inside = (cells >> 7) & 3
        parts = []
        for part in range(2):
            total = jnp.zeros((8, LANES), F32)
            for number in range(4):
                line = jnp.broadcast_to(wind[pl.ds(part * ROWS + base + number, 1), :], (8, LANES))
                total = jnp.where(inside == number, gathered(line, lane), total)
            parts.append(total[0:1])
        return parts

    def back(chunk, target, held):
        return pltpu.make_async_remote_copy(
            returning.at[chunk, target], held.at[me], send_sem.at[2 + chunk], back_sem.at[(1 + (me >> 3)) * chunk],
            device_id={"comp": target}, device_id_type=MESH)

    def source_terms(chunk, held):
        landed = incoming.at[chunk, pl.ds(0, COMPS - 1)]
        pltpu.make_async_copy(landed, landed, forward_sem.at[chunk]).wait()
        wind_u, wind_v = wind_at(unit_row(chunk, me))

        def collect(source, total):
            values = incoming[chunk, source]
            dense[pl.ds(source * LOCAL, LOCAL), :] = values
            return total + omega[source] * values

        total = lax.fori_loop(0, COMPS, collect, jnp.zeros((LOCAL, LANES), F32), unroll=True)
        energy = jnp.sum(total, axis=0, keepdims=True) * energy_scale()
        loss = dissipation * energy * energy
        rounded[...] = dense[0:SPEC, :].astype(jnp.bfloat16)

        @pl.loop(0, SPEC // TILE)
        def _(tile):
            rows = pl.ds(pl.multiple_of(tile * TILE, TILE), TILE)
            coupled[rows, :] = jnp.dot(kernel_buf[rows, :], rounded[...], preferred_element_type=F32)

        def updated(target):
            points = incoming[chunk, target]
            speed = omega[target]
            along = cosine[target] * wind_u + sine[target] * wind_v
            growth = growth_rate * speed * jnp.maximum(along - wind_floor, 0.0)
            damping = speed * speed * loss
            joined = coupled[pl.ds(target * LOCAL, LOCAL), :]
            return points + points * (growth - damping + coupling * joined) / (1.0 + damping)

        held[me] = updated(me)
        return updated

    updated = source_terms(1, arrived_b)

    @pl.loop(1, EARLY)
    def _(step):
        target = shifted(me, step)
        returning[1, target] = updated(target)
        back(1, target, arrived_b).start()

    @pl.loop(EARLY, COMPS)
    def _(step):
        target = shifted(me, step)
        returning[1, target] = updated(target)

    updated_later = source_terms(0, arrived_a)

    @pl.loop(1, COMPS)
    def _(step):
        target = shifted(me, step)
        returning[0, target] = updated_later(target)
        back(0, target, arrived_a).start()

    @pl.loop(EARLY, COMPS)
    def _(step):
        back(1, shifted(me, step), arrived_b).start()

    landed = arrived_a.at[pl.ds(0, COMPS - 1)]
    pltpu.make_async_copy(landed, landed, back_sem.at[0]).wait()

    @pl.loop(0, BLOCKS)
    def _(block):
        first_unit = units_smem[4, block]
        pieces = []
        for number in range(4):
            line = pl.ds(block * 4 + number, 1)
            lane, part = spread_rows(lane_map[line, :]), spread_rows(part_map[line, :])
            total = jnp.zeros((LOCAL, LANES), F32)
            for offset in range(3):
                values = arrived_a[jnp.clip(first_unit + offset, 0, COMPS - 1)]
                total = jnp.where(part == offset + 1, gathered(values, lane), total)
            pieces.append(total)
        for number in range(4):
            expanded[block * 4 + number] = pieces[number]

    def finish(block):
        values = arrived_b[block]
        for number in range(4):
            x = block * 4 + number
            line = pl.ds(x, 1)
            lane, part = spread_rows(lane_map[line, :]), spread_rows(part_map[line, :])
            piece = jnp.where(part == 0, gathered(values, lane), expanded[x])
            result[pl.ds(x, LOCAL, stride=ROWS), :] = piece

    for step in range(8):
        plane = ((me >> 3) + 8 - step) & 7
        landed = arrived_b.at[pl.ds(0, 8 if step else 7)]
        pltpu.make_async_copy(landed, landed, back_sem.at[1 + plane]).wait()

        @pl.loop(0, 8, unroll=4)
        def _(place, plane=plane):
            finish(plane * 8 + place)

    for number in range(4):
        sent = outgoing.at[0, pl.ds(0, COMPS - 1)]
        pltpu.make_async_copy(sent, sent, send_sem.at[number]).wait()


def on_device(spectrum, wind, sea_table, transfer_kernel):
    table, scalars = (jnp.asarray(array) for array in component_tables())
    anywhere = pl.BlockSpec(memory_space=pltpu.HBM)
    wave = pltpu.VMEM((PADDED_COMP * STRIDE, LANES), F32)
    line_map = pltpu.VMEM((PADDED_ROWS, LANES), jnp.int32)
    per_source = pltpu.VMEM((COMPS, LOCAL, LANES), F32)
    per_chunk = pltpu.VMEM((2, COMPS, LOCAL, LANES), F32)
    rim = pltpu.VMEM((3, LOCAL, LANES), F32)
    dense = pltpu.VMEM((PADDED_SPEC, LANES), F32)
    dma = pltpu.SemaphoreType.DMA
    result = pl.pallas_call(
        exchange_kernel,
        out_shape=pltpu.VMEM((PADDED_COMP * ROWS, LANES), F32),
        in_specs=[anywhere] * 6,
        out_specs=pl.BlockSpec(memory_space=pltpu.VMEM),
        scratch_shapes=[
            wave,
            wave,
            wave,
            pltpu.VMEM((BLOCKS, 4 * LANES), jnp.int32),
            pltpu.VMEM((PADDED_ROWS, LANES), F32),
            line_map,
            line_map,
            line_map,
            pltpu.VMEM((8, LANES), jnp.int32),
            pltpu.SMEM((8, LANES), jnp.int32),
            pltpu.SMEM((8, LANES), F32),
            pltpu.VMEM((2 * ROWS + 8, LANES), F32),
            pltpu.VMEM((SPEC, SPEC), jnp.bfloat16),
            per_source,
            pltpu.VMEM((LOCAL, LANES), F32),
            per_source,
            per_source,
            per_source,
            rim,
            rim,
            rim,
            rim,
            per_chunk,
            per_chunk,
            dense,
            pltpu.VMEM((SPEC, LANES), jnp.bfloat16),
            dense,
            per_chunk,
            per_source,
            per_source,
            pltpu.VMEM((ROWS, LOCAL, LANES), F32),
            dma((7,)),
            dma((LOCAL // SHARE,)),
            dma((2,)),
            dma((2,)),
            dma((4,)),
            dma((2,)),
            dma((9,)),
        ],
        compiler_params=pltpu.CompilerParams(
            collective_id=0, has_side_effects=True, vmem_limit_bytes=59 * 1024 * 1024
        ),
        cost_estimate=pl.CostEstimate(flops=2 * SPEC * SPEC * 256, bytes_accessed=16 << 20, transcendentals=0),
        name="exchange",
    )(spectrum, wind.reshape(2 * ROWS, LANES), sea_table, transfer_kernel, table, scalars)
    return result[: LOCAL * ROWS].reshape(LOCAL, ROWS, LANES)


def solution(mesh):
    placed = (P("comp", "region", None), P(None, "region", None), P("region", None), P())
    return jax.shard_map(
        on_device, mesh=mesh, in_specs=placed, out_specs=P("comp", "region", None), check_vma=False
    )
```

time: 113 us -> 102 us (0.903)
  Pallas kernels: 108 us -> 100 us
  local copies, waits for them, and re-layouts: 4.17 us -> 2.02 us
    pallas_call x1, Pallas kernels: 108 us -> 100 us  [on_device(): pl.pallas_call(exchange_kernel, out_shape=pltpu.VMEM((PADDED_COMP * ROWS,...]
    unnamed x1 -> x0, local copies, waits for them, and re-layouts: 4.17 us -> none
    slice x0 -> x1, local copies, waits for them, and re-layouts: none -> 2.02 us  [on_device(): return result[:LOCAL * ROWS].reshape(LOCAL, ROWS, LANES)]
where the time goes in v3:
time: 102 us
  Pallas kernels  100 us (98%)
  local copies, waits for them, and re-layouts  2.02 us (2%)
    pallas_call x1, Pallas kernels, on_device(): pl.pallas_call(exchange_kernel, out_shape=pltpu.VMEM((PADDED_COMP * ROWS,...  100 us

profile of v3, /device:TPU:1, one launch (start us, length us, event | category | flops | bytes accessed | tf_op | source)
XLA Modules:
  0.0 102.2 jit_solution(18340858818139197301)
XLA Ops:
  0.0 100.2 %exchange.1 = f32[8192,128]{1,0:T(8,128)S(1)} custom-call(f32[27,256,128]{2,1,0:T(8,128)} %spectrum.1, f32[512,128]{1,0:T(8,128)} %bitcast.2, s32[64,512]{1,0:T(8,128)} %listed.1, bf16[1728,1728]{1,0:T(8,128)(2,1)} %transfer.1, f32[64,27,128]{2,1,0:T(8,128)} %constant.4.clone.table, f32[64,8,128]{2,1,0:T(8,128)} %constant.5.clone.scalars), custom_call_target="tpu_custom_call" | custom-call | flops 1528823808 | bytes 16777216 | tf_op jit(solution)/shard_map/exchange/pallas_call | solution.py:449
  100.2 2.0 %slice.3 = f32[6912,128]{1,0:T(8,128)} slice(f32[8192,128]{1,0:T(8,128)S(1)} %exchange.1), slice={[0:6912], [0:128]} | slice | bytes 7077888 | tf_op jit(solution)/shard_map/slice | solution.py:500

commit v4 on v3

--- a/solution.py
+++ b/solution.py
@@ -22,7 +22,7 @@
 PADDED_COMP = 32
 PADDED_SPEC = SPEC + 32
 TILE = 432
-EARLY = 20
+EARLY = 1
 SHARE = 9
 F32 = jnp.float32
 MESH = pl.DeviceIdType.MESH
@@ -60,6 +60,15 @@
     z = ((me & 56) + (step & 56)) & 56
     y = ((me & 6) + (step & 6)) & 6
     return z + y + ((me + step) & 1)
+
+
+def quarter_of(me, number):
+    order = jnp.where(number == 2, 3, jnp.where(number == 3, 0, 2 - number))
+    return ((me >> 4) + order) & 3
+
+
+def device_in(me, quarter, place):
+    return quarter * 16 + ((me ^ place ^ 8) & 8) + ((me + place) & 7)
 
 
 def gathered(source, lanes):
@@ -187,7 +196,9 @@
                 changed = centre_w * here + x_w * beside + y_w * pltpu.roll(here, turn, 1)
                 target[pl.ds(base, 8), :] = mask[pl.ds(row, 8), :] * changed
 
-    substep(wave0, wave1, range(ROWS // 8), 3)
+    first_quarter = quarter_of(me, 0)
+    needed = jnp.clip(first_quarter * 64 - 8, 0, ROWS - 80)
+    substep(wave0, wave1, range(10), 9, origin=needed)
 
     def packed(row):
         cells = sea_rows[pl.ds(row, 1), :]
@@ -211,20 +222,21 @@
         outgoing[chunk, target] = packed(unit_row(chunk, target))
         forward(chunk, target).start()
 
-    def quarter_sends(number, order):
-        part = ((me >> 4) + order) & 3
-        substep(wave1, wave2, range(8), 9, origin=part * 64)
+    def quarter_sends(number):
+        quarter = quarter_of(me, number)
+        substep(wave1, wave2, range(8), 9, origin=quarter * 64)
 
         @pl.loop(0, 16)
         def _(place):
-            target = part * 16 + ((me + place) & 15)
+            target = device_in(me, quarter, place)
             ready = (target >= 4) & (target < BLOCKS - 4) if number == 0 else target != me
 
             @pl.when(ready)
             def _():
                 send(1, target)
 
-    quarter_sends(0, 2)
+    quarter_sends(0)
+    substep(wave0, wave1, range(ROWS // 8), 3)
     load_kernel.start()
     load_constants.start()
     load_wind.start()
@@ -258,7 +270,7 @@
     halo(from_east, region < REGIONS - 1, last_row, False)
     substep(wave0, wave1, (0, ROWS // 8 - 1), 9)
     substep(wave1, wave2, (0, ROWS // 8 - 1), 9)
-    quarter_sends(1, 1)
+    quarter_sends(1)
 
     row_number = lax.broadcasted_iota(jnp.int32, (ROWS, LANES), 0)
     lane_position = lax.broadcasted_iota(jnp.int32, (ROWS, LANES), 1)
@@ -276,22 +288,28 @@
     load_units = pltpu.make_async_copy(units, units_smem, load_sem.at[5])
     load_units.start()
 
-    quarter_sends(2, 3)
-    quarter_sends(3, 0)
+    quarter_sends(2)
+    quarter_sends(3)
+
+    @pl.when((first_quarter == 0) | (first_quarter == 3))
+    def _():
+        @pl.loop(0, 4)
+        def _(place):
+            send(1, first_quarter * 20 + ((me + place) & 3))
+
+    load_units.wait()
 
     @pl.loop(0, 4)
-    def _(place):
-        part = ((me >> 4) + 2) & 3
-
-        @pl.when((part == 0) | (part == 3))
-        def _():
-            send(1, part * 20 + ((me + place) & 3))
-
-    load_units.wait()
-
-    @pl.loop(1, COMPS)
-    def _(step):
-        send(0, shifted(me, step))
+    def _(number):
+        quarter = quarter_of(me, number)
+
+        @pl.loop(0, 16)
+        def _(place):
+            target = device_in(me, quarter, place)
+
+            @pl.when(target != me)
+            def _():
+                send(0, target)
 
     for chunk in range(2):
         incoming[chunk, me] = packed(unit_row(chunk, me))
@@ -335,7 +353,7 @@
 
     def back(chunk, target, held):
         return pltpu.make_async_remote_copy(
-            returning.at[chunk, target], held.at[me], send_sem.at[2 + chunk], back_sem.at[(1 + (me >> 3)) * chunk],
+            returning.at[chunk, target], held.at[me], send_sem.at[2 + chunk], back_sem.at[chunk, me >> 3],
             device_id={"comp": target}, device_id_type=MESH)
 
     def source_terms(chunk, held):
@@ -352,11 +370,6 @@
         energy = jnp.sum(total, axis=0, keepdims=True) * energy_scale()
         loss = dissipation * energy * energy
         rounded[...] = dense[0:SPEC, :].astype(jnp.bfloat16)
-
-        @pl.loop(0, SPEC // TILE)
-        def _(tile):
-            rows = pl.ds(pl.multiple_of(tile * TILE, TILE), TILE)
-            coupled[rows, :] = jnp.dot(kernel_buf[rows, :], rounded[...], preferred_element_type=F32)
 
         def updated(target):
             points = incoming[chunk, target]
@@ -367,69 +380,96 @@
             joined = coupled[pl.ds(target * LOCAL, LOCAL), :]
             return points + points * (growth - damping + coupling * joined) / (1.0 + damping)
 
-        held[me] = updated(me)
-        return updated
-
-    updated = source_terms(1, arrived_b)
-
-    @pl.loop(1, EARLY)
-    def _(step):
-        target = shifted(me, step)
-        returning[1, target] = updated(target)
-        back(1, target, arrived_b).start()
-
-    @pl.loop(EARLY, COMPS)
-    def _(step):
-        target = shifted(me, step)
-        returning[1, target] = updated(target)
-
-    updated_later = source_terms(0, arrived_a)
-
-    @pl.loop(1, COMPS)
-    def _(step):
-        target = shifted(me, step)
-        returning[0, target] = updated_later(target)
-        back(0, target, arrived_a).start()
-
-    @pl.loop(EARLY, COMPS)
-    def _(step):
-        back(1, shifted(me, step), arrived_b).start()
-
-    landed = arrived_a.at[pl.ds(0, COMPS - 1)]
-    pltpu.make_async_copy(landed, landed, back_sem.at[0]).wait()
-
-    @pl.loop(0, BLOCKS)
-    def _(block):
-        first_unit = units_smem[4, block]
-        pieces = []
-        for number in range(4):
-            line = pl.ds(block * 4 + number, 1)
-            lane, part = spread_rows(lane_map[line, :]), spread_rows(part_map[line, :])
-            total = jnp.zeros((LOCAL, LANES), F32)
-            for offset in range(3):
-                values = arrived_a[jnp.clip(first_unit + offset, 0, COMPS - 1)]
-                total = jnp.where(part == offset + 1, gathered(values, lane), total)
-            pieces.append(total)
-        for number in range(4):
-            expanded[block * 4 + number] = pieces[number]
+        def update(number, sending):
+            quarter = quarter_of(me, number)
+            rows = pl.ds(pl.multiple_of(quarter * TILE, TILE), TILE)
+            coupled[rows, :] = jnp.dot(kernel_buf[rows, :], rounded[...], preferred_element_type=F32)
+
+            @pl.loop(0, 16, unroll=2)
+            def _(place):
+                target = device_in(me, quarter, place)
+                values = updated(target)
+                returning[chunk, target] = values
+
+                @pl.when(target == me)
+                def _():
+                    held[me] = values
+
+                if sending:
+
+                    @pl.when(target != me)
+                    def _():
+                        back(chunk, target, held).start()
+
+        return update
+
+    update = source_terms(1, arrived_b)
+
+    @pl.loop(0, EARLY)
+    def _(number):
+        update(number, True)
+
+    @pl.loop(EARLY, 4)
+    def _(number):
+        update(number, False)
+
+    update_later = source_terms(0, arrived_a)
+
+    @pl.loop(0, 4)
+    def _(number):
+        update_later(number, True)
+
+    @pl.loop(EARLY, 4)
+    def _(number):
+        quarter = quarter_of(me, number)
+
+        @pl.loop(0, 16)
+        def _(place):
+            target = device_in(me, quarter, place)
+
+            @pl.when(target != me)
+            def _():
+                back(1, target, arrived_b).start()
+
+    def plane_of(number):
+        shift = (4, 4, 2, 2, 6, 6, 0, 0)[number]
+        return (((me >> 3) + 8 - shift) & 6) + (((me >> 3) + number + 1) & 1)
+
+    def arrival(number, chunk, held):
+        landed = held.at[pl.ds(0, 8 if number < 7 else 7)]
+        pltpu.make_async_copy(landed, landed, back_sem.at[chunk, plane_of(number)]).wait()
+
+    for number in range(8):
+        arrival(number, 0, arrived_a)
+
+        @pl.loop(0, 8, unroll=4)
+        def _(place, number=number):
+            unit = plane_of(number) * 8 + place
+            base = jnp.clip(units_smem[0, unit], 0, ROWS - 1) & ~3
+            values = arrived_a[unit]
+            for line in range(4):
+                lane = spread_rows(lane_map[pl.ds(base + line, 1), :])
+                expanded[unit * 4 + line] = gathered(values, lane)
 
     def finish(block):
         values = arrived_b[block]
+        first_unit = units_smem[4, block]
         for number in range(4):
             x = block * 4 + number
             line = pl.ds(x, 1)
             lane, part = spread_rows(lane_map[line, :]), spread_rows(part_map[line, :])
-            piece = jnp.where(part == 0, gathered(values, lane), expanded[x])
+            piece = jnp.where(part == 0, gathered(values, lane), 0.0)
+            for offset in range(3):
+                unit = jnp.clip(first_unit + offset, 0, COMPS - 1)
+                piece = jnp.where(part == offset + 1, expanded[unit * 4 + number], piece)
             result[pl.ds(x, LOCAL, stride=ROWS), :] = piece
 
-    for step in range(8):
-        plane = ((me >> 3) + 8 - step) & 7
-        landed = arrived_b.at[pl.ds(0, 8 if step else 7)]
-        pltpu.make_async_copy(landed, landed, back_sem.at[1 + plane]).wait()
+    for number in range(8):
+        arrival(number, 1, arrived_b)
 
         @pl.loop(0, 8, unroll=4)
-        def _(place, plane=plane):
-            finish(plane * 8 + place)
+        def _(place, number=number):
+            finish(plane_of(number) * 8 + place)
 
     for number in range(4):
         sent = outgoing.at[0, pl.ds(0, COMPS - 1)]
@@ -489,7 +529,7 @@
             dma((2,)),
             dma((4,)),
             dma((2,)),
-            dma((9,)),
+            dma((2, 8)),
         ],
         compiler_params=pltpu.CompilerParams(
             collective_id=0, has_side_effects=True, vmem_limit_bytes=59 * 1024 * 1024

time: 102 us -> 98.3 us (0.964)
  Pallas kernels: 100 us -> 96.2 us
    pallas_call x1, Pallas kernels: 100 us -> 96.2 us  [on_device(): pl.pallas_call(exchange_kernel, out_shape=pltpu.VMEM((PADDED_COMP * ROWS,...]
where the time goes in v4:
time: 98.3 us; the launch traced here: 98.2 us
  Pallas kernels  96.2 us (98%)
  local copies, waits for them, and re-layouts  2.02 us (2%)
    pallas_call x1, Pallas kernels, on_device(): pl.pallas_call(exchange_kernel, out_shape=pltpu.VMEM((PADDED_COMP * ROWS,...  96.2 us
    slice x1, local copies, waits for them, and re-layouts, on_device(): return result[:LOCAL * ROWS].reshape(LOCAL, ROWS, LANES)  2.02 us

profile of v4, /device:TPU:1, one launch (start us, length us, event | category | flops | bytes accessed | tf_op | source)
XLA Modules:
  0.0 98.2 jit_solution(14121979946208613465)
XLA Ops:
  0.0 96.2 %exchange.1 = f32[8192,128]{1,0:T(8,128)S(1)} custom-call(f32[27,256,128]{2,1,0:T(8,128)} %spectrum.1, f32[512,128]{1,0:T(8,128)} %bitcast.2, s32[64,512]{1,0:T(8,128)} %listed.1, bf16[1728,1728]{1,0:T(8,128)(2,1)} %transfer.1, f32[64,27,128]{2,1,0:T(8,128)} %constant.4.clone.table, f32[64,8,128]{2,1,0:T(8,128)} %constant.5.clone.scalars), custom_call_target="tpu_custom_call" | custom-call | flops 1528823808 | bytes 16777216 | tf_op jit(solution)/shard_map/exchange/pallas_call | solution.py:489
  96.2 2.0 %slice.3 = f32[6912,128]{1,0:T(8,128)} slice(f32[8192,128]{1,0:T(8,128)S(1)} %exchange.1), slice={[0:6912], [0:128]} | slice | bytes 7077888 | tf_op jit(solution)/shard_map/slice | solution.py:540

commit v5 on v4

--- a/solution.py
+++ b/solution.py
@@ -137,23 +137,39 @@
     def block_rows(block):
         return pl.ds(pl.multiple_of(block * 4, 4), 4)
 
-    @pl.loop(0, BLOCKS, unroll=8)
-    def _(block):
+    def mask_block(block):
         mask[block_rows(block), :] = listed_maps(block, [1.0])[0:4]
 
     def strided(x):
         return pl.ds(x, LOCAL, stride=STRIDE)
+
+    def masked(comp, start, count):
+        rows = pl.ds(pl.multiple_of(comp * STRIDE + 8 + start, 8), count)
+        wave0[rows, :] = mask[pl.ds(pl.multiple_of(start, 8), count), :] * wave0[rows, :]
+
+    first_quarter = quarter_of(me, 0)
+
+    def rows_for(number):
+        return jnp.clip(quarter_of(me, number) * 64 - 8, 0, ROWS - 80)
+
+    def quarter_mask(number):
+        @pl.loop(0, 20, unroll=10)
+        def _(place):
+            mask_block((rows_for(number) >> 2) + place)
+
+    quarter_mask(0)
+    for block in (0, 1, BLOCKS - 2, BLOCKS - 1):
+        mask_block(block)
 
     for share in range(LOCAL // SHARE):
         landed = wave0.at[pl.ds(0, SHARE * ROWS)]
         pltpu.make_async_copy(landed, landed, comp_sem.at[share]).wait()
 
-        @pl.loop(share * SHARE, (share + 1) * SHARE)
+        @pl.loop(share * SHARE, (share + 1) * SHARE, unroll=3)
         def _(comp):
-            base = pl.multiple_of(comp * STRIDE + 8, 8)
-            for start in range(0, ROWS, 64):
-                rows = pl.ds(base + start, 64)
-                wave0[rows, :] = mask[start : start + 64, :] * wave0[rows, :]
+            masked(comp, rows_for(0), 80)
+            masked(comp, 0, 8)
+            masked(comp, ROWS - 8, 8)
 
     nothing = jnp.zeros((LOCAL, LANES), F32)
     for wave in (wave0, wave1):
@@ -167,14 +183,6 @@
     to_east[0] = last_row
     to_east[1] = wave0[strided(6 + ROWS), :]
     to_east[2] = spread_rows(mask[ROWS - 1 : ROWS, :])
-    pl.semaphore_wait(barrier, COMPS + 1)
-    send_west = pltpu.make_async_remote_copy(
-        to_west, from_east, halo_send.at[0], halo_recv.at[0], device_id={"region": west}, device_id_type=MESH)
-    send_east = pltpu.make_async_remote_copy(
-        to_east, from_west, halo_send.at[1], halo_recv.at[1], device_id={"region": east}, device_id_type=MESH)
-    send_west.start()
-    send_east.start()
-
     load_scalars.wait()
     lanes = lax.broadcasted_iota(jnp.int32, (8, LANES), 1)
 
@@ -196,9 +204,7 @@
                 changed = centre_w * here + x_w * beside + y_w * pltpu.roll(here, turn, 1)
                 target[pl.ds(base, 8), :] = mask[pl.ds(row, 8), :] * changed
 
-    first_quarter = quarter_of(me, 0)
-    needed = jnp.clip(first_quarter * 64 - 8, 0, ROWS - 80)
-    substep(wave0, wave1, range(10), 9, origin=needed)
+    substep(wave0, wave1, range(10), 9, origin=rows_for(0))
 
     def packed(row):
         cells = sea_rows[pl.ds(row, 1), :]
@@ -222,9 +228,11 @@
         outgoing[chunk, target] = packed(unit_row(chunk, target))
         forward(chunk, target).start()
 
+    def quarter_step(number):
+        substep(wave1, wave2, range(8), 9, origin=quarter_of(me, number) * 64)
+
     def quarter_sends(number):
         quarter = quarter_of(me, number)
-        substep(wave1, wave2, range(8), 9, origin=quarter * 64)
 
         @pl.loop(0, 16)
         def _(place):
@@ -235,8 +243,27 @@
             def _():
                 send(1, target)
 
+    quarter_step(0)
+    pl.semaphore_wait(barrier, COMPS + 1)
+    send_west = pltpu.make_async_remote_copy(
+        to_west, from_east, halo_send.at[0], halo_recv.at[0], device_id={"region": west}, device_id_type=MESH)
+    send_east = pltpu.make_async_remote_copy(
+        to_east, from_west, halo_send.at[1], halo_recv.at[1], device_id={"region": east}, device_id_type=MESH)
+    send_west.start()
+    send_east.start()
+
     quarter_sends(0)
-    substep(wave0, wave1, range(ROWS // 8), 3)
+
+    def prepare(number):
+        quarter_mask(number)
+
+        @pl.loop(0, LOCAL, unroll=3)
+        def _(comp):
+            masked(comp, rows_for(number), 80)
+
+        substep(wave0, wave1, range(10), 9, origin=rows_for(number))
+
+    prepare(1)
     load_kernel.start()
     load_constants.start()
     load_wind.start()
@@ -270,6 +297,7 @@
     halo(from_east, region < REGIONS - 1, last_row, False)
     substep(wave0, wave1, (0, ROWS // 8 - 1), 9)
     substep(wave1, wave2, (0, ROWS // 8 - 1), 9)
+    quarter_step(1)
     quarter_sends(1)
 
     row_number = lax.broadcasted_iota(jnp.int32, (ROWS, LANES), 0)
@@ -288,7 +316,11 @@
     load_units = pltpu.make_async_copy(units, units_smem, load_sem.at[5])
     load_units.start()
 
+    prepare(2)
+    quarter_step(2)
     quarter_sends(2)
+    prepare(3)
+    quarter_step(3)
     quarter_sends(3)
 
     @pl.when((first_quarter == 0) | (first_quarter == 3))

time: 98.3 us -> 97.6 us (level)
  no operation moved by 1% of the time
where the time goes in v5:
time: 97.6 us; the launch traced here: 97.5 us
  Pallas kernels  95.5 us (98%)
  local copies, waits for them, and re-layouts  2.02 us (2%)
    pallas_call x1, Pallas kernels, on_device(): pl.pallas_call(exchange_kernel, out_shape=pltpu.VMEM((PADDED_COMP * ROWS,...  95.5 us
    slice x1, local copies, waits for them, and re-layouts, on_device(): return result[:LOCAL * ROWS].reshape(LOCAL, ROWS, LANES)  2.02 us

profile of v5, /device:TPU:1, one launch (start us, length us, event | category | flops | bytes accessed | tf_op | source)
XLA Modules:
  0.0 97.5 jit_solution(1047375992273975925)
XLA Ops:
  0.0 95.5 %exchange.1 = f32[8192,128]{1,0:T(8,128)S(1)} custom-call(f32[27,256,128]{2,1,0:T(8,128)} %spectrum.1, f32[512,128]{1,0:T(8,128)} %bitcast.2, s32[64,512]{1,0:T(8,128)} %listed.1, bf16[1728,1728]{1,0:T(8,128)(2,1)} %transfer.1, f32[64,27,128]{2,1,0:T(8,128)} %constant.4.clone.table, f32[64,8,128]{2,1,0:T(8,128)} %constant.5.clone.scalars), custom_call_target="tpu_custom_call" | custom-call | flops 1528823808 | bytes 16777216 | tf_op jit(solution)/shard_map/exchange/pallas_call | solution.py:521
  95.5 2.0 %slice.3 = f32[6912,128]{1,0:T(8,128)} slice(f32[8192,128]{1,0:T(8,128)S(1)} %exchange.1), slice={[0:6912], [0:128]} | slice | bytes 7077888 | tf_op jit(solution)/shard_map/slice | solution.py:572

commit v6 on v5

--- a/solution.py
+++ b/solution.py
@@ -221,7 +221,7 @@
 
     def forward(chunk, target):
         return pltpu.make_async_remote_copy(
-            outgoing.at[chunk, target], incoming.at[chunk, me], send_sem.at[chunk], forward_sem.at[chunk],
+            outgoing.at[chunk, target], incoming.at[chunk, me], send_sem.at[chunk], forward_sem.at[chunk, me >> 4],
             device_id={"comp": target}, device_id_type=MESH)
 
     def send(chunk, target):
@@ -389,19 +389,21 @@
             device_id={"comp": target}, device_id_type=MESH)
 
     def source_terms(chunk, held):
-        landed = incoming.at[chunk, pl.ds(0, COMPS - 1)]
-        pltpu.make_async_copy(landed, landed, forward_sem.at[chunk]).wait()
         wind_u, wind_v = wind_at(unit_row(chunk, me))
-
-        def collect(source, total):
-            values = incoming[chunk, source]
-            dense[pl.ds(source * LOCAL, LOCAL), :] = values
-            return total + omega[source] * values
-
-        total = lax.fori_loop(0, COMPS, collect, jnp.zeros((LOCAL, LANES), F32), unroll=True)
+        total = jnp.zeros((LOCAL, LANES), F32)
+        for number, turn in enumerate((2, 1, 3, 0)):
+            quarter = ((me >> 4) + 4 - turn) & 3
+            landed = incoming.at[chunk, pl.ds(0, 16 if number < 3 else 15)]
+            pltpu.make_async_copy(landed, landed, forward_sem.at[chunk, quarter]).wait()
+            start = pl.multiple_of(quarter * TILE, TILE)
+            for place in range(16):
+                values = incoming[chunk, quarter * 16 + place]
+                dense[pl.ds(start + place * LOCAL, LOCAL), :] = values
+                total = total + omega[quarter * 16 + place] * values
+            rounded[pl.ds(start, TILE), :] = dense[pl.ds(start, TILE), :].astype(jnp.bfloat16)
+
         energy = jnp.sum(total, axis=0, keepdims=True) * energy_scale()
         loss = dissipation * energy * energy
-        rounded[...] = dense[0:SPEC, :].astype(jnp.bfloat16)
 
         def updated(target):
             points = incoming[chunk, target]
@@ -417,7 +419,7 @@
             rows = pl.ds(pl.multiple_of(quarter * TILE, TILE), TILE)
             coupled[rows, :] = jnp.dot(kernel_buf[rows, :], rounded[...], preferred_element_type=F32)
 
-            @pl.loop(0, 16, unroll=2)
+            @pl.loop(0, 16, unroll=4)
             def _(place):
                 target = device_in(me, quarter, place)
                 values = updated(target)
@@ -560,7 +562,7 @@
             dma((2,)),
             dma((2,)),
             dma((4,)),
-            dma((2,)),
+            dma((2, 4)),
             dma((2, 8)),
         ],
         compiler_params=pltpu.CompilerParams(

time: 97.6 us -> 97.7 us (level)
  no operation moved by 1% of the time
where the time goes in v6:
time: 97.7 us; the launch traced here: 97.6 us
  Pallas kernels  95.5 us (98%)
  local copies, waits for them, and re-layouts  2.02 us (2%)
    pallas_call x1, Pallas kernels, on_device(): pl.pallas_call(exchange_kernel, out_shape=pltpu.VMEM((PADDED_COMP * ROWS,...  95.5 us
    slice x1, local copies, waits for them, and re-layouts, on_device(): return result[:LOCAL * ROWS].reshape(LOCAL, ROWS, LANES)  2.02 us

profile of v6, /device:TPU:1, one launch (start us, length us, event | category | flops | bytes accessed | tf_op | source)
XLA Modules:
  0.0 97.6 jit_solution(3389940484972848756)
XLA Ops:
  0.0 95.5 %exchange.1 = f32[8192,128]{1,0:T(8,128)S(1)} custom-call(f32[27,256,128]{2,1,0:T(8,128)} %spectrum.1, f32[512,128]{1,0:T(8,128)} %bitcast.2, s32[64,512]{1,0:T(8,128)} %listed.1, bf16[1728,1728]{1,0:T(8,128)(2,1)} %transfer.1, f32[64,27,128]{2,1,0:T(8,128)} %constant.4.clone.table, f32[64,8,128]{2,1,0:T(8,128)} %constant.5.clone.scalars), custom_call_target="tpu_custom_call" | custom-call | flops 1528823808 | bytes 16777216 | tf_op jit(solution)/shard_map/exchange/pallas_call | solution.py:523
  95.5 2.0 %slice.3 = f32[6912,128]{1,0:T(8,128)} slice(f32[8192,128]{1,0:T(8,128)S(1)} %exchange.1), slice={[0:6912], [0:128]} | slice | bytes 7077888 | tf_op jit(solution)/shard_map/slice | solution.py:574

commit v7 on v6

--- a/solution.py
+++ b/solution.py
@@ -501,7 +501,7 @@
     for number in range(8):
         arrival(number, 1, arrived_b)
 
-        @pl.loop(0, 8, unroll=4)
+        @pl.loop(0, 8, unroll=8)
         def _(place, number=number):
             finish(plane_of(number) * 8 + place)
 

time: 97.7 us -> 97.5 us (level)
  no operation moved by 1% of the time
where the time goes in v7:
time: 97.5 us; the launch traced here: 97.4 us
  Pallas kernels  95.4 us (98%)
  local copies, waits for them, and re-layouts  2.02 us (2%)
    pallas_call x1, Pallas kernels, on_device(): pl.pallas_call(exchange_kernel, out_shape=pltpu.VMEM((PADDED_COMP * ROWS,...  95.4 us
    slice x1, local copies, waits for them, and re-layouts, on_device(): return result[:LOCAL * ROWS].reshape(LOCAL, ROWS, LANES)  2.02 us

profile of v7, /device:TPU:1, one launch (start us, length us, event | category | flops | bytes accessed | tf_op | source)
XLA Modules:
  0.0 97.4 jit_solution(17306570579217854734)
XLA Ops:
  0.0 95.4 %exchange.1 = f32[8192,128]{1,0:T(8,128)S(1)} custom-call(f32[27,256,128]{2,1,0:T(8,128)} %spectrum.1, f32[512,128]{1,0:T(8,128)} %bitcast.2, s32[64,512]{1,0:T(8,128)} %listed.1, bf16[1728,1728]{1,0:T(8,128)(2,1)} %transfer.1, f32[64,27,128]{2,1,0:T(8,128)} %constant.4.clone.table, f32[64,8,128]{2,1,0:T(8,128)} %constant.5.clone.scalars), custom_call_target="tpu_custom_call" | custom-call | flops 1528823808 | bytes 16777216 | tf_op jit(solution)/shard_map/exchange/pallas_call | solution.py:523
  95.4 2.0 %slice.3 = f32[6912,128]{1,0:T(8,128)} slice(f32[8192,128]{1,0:T(8,128)S(1)} %exchange.1), slice={[0:6912], [0:128]} | slice | bytes 7077888 | tf_op jit(solution)/shard_map/slice | solution.py:574
